TPU v7x, 256 devices: a whole 4x4x8 slice. The times are simulated.
256 devices in a mesh: row: 16 (over x, z_lo), col: 16 (over z_hi, y, core).
Axes of the slice: x: 4, y: 4, z: 8 (z_hi: 2, z_lo: 4; z = z_hi * 4 + z_lo), core: 2. Of those that a mesh axis runs over, the one named last changes fastest.
Arguments:
- pair_block: bfloat16 [1024, 2048, 128], P('row', 'col'), may hold values from -6 to 6
- left_panel: bfloat16 [1024, 512, 128], P('row', 'col'), may hold values from -6 to 6
- right_panel: bfloat16 [2048, 512, 128], P('col', 'row'), may hold values from -6 to 6
- mask_left: int32 [1024, 512], P('row', 'col'), may hold values 0 or 1
- mask_right: int32 [2048, 512], P('col', 'row'), may hold values 0 or 1
- in_gain: float32 [128], replicated, may hold values from 0.1 to 1.9
- in_bias: float32 [128], replicated, may hold values from -3 to 3
- w_in: bfloat16 [128, 512], replicated, may hold values from -0.5 to 0.5
- out_gain: float32 [128], replicated, may hold values from 0.1 to 1.9
- out_bias: float32 [128], replicated, may hold values from -3 to 3
- w_gate_out: bfloat16 [128, 128], replicated, may hold values from -0.5 to 0.5
- w_out: bfloat16 [128, 128], replicated, may hold values from -0.5 to 0.5
Outputs:
- update: bfloat16 [1024, 2048, 128], P('row', 'col')
All inputs are finite; a program needn't handle non-finite values. No bound on the sum of `mask_left` or of `mask_right` on one device may be relied on, other than what follows from the above.
Results may differ from a plain program's by a relative error of at most 0.0058.
Values may be sent and summed in bfloat16 or wider, within the bound.
No kernel may reach another device: no remote copies, remote signals or barrier semaphores. Data moves between devices by JAX's collectives and lax.ppermute only.
A program may use at most 128 MiB of HBM per device.

v0:
```python
import jax
import jax.numpy as jnp
from jax import lax
from jax.sharding import PartitionSpec as P


def layer_norm(value, gain, bias):
    value = value.astype(jnp.float32)
    center = value - jnp.mean(value, axis=-1, keepdims=True)
    spread = jnp.mean(center * center, axis=-1, keepdims=True)
    return center * lax.rsqrt(spread + 1e-05) * gain + bias


def gated_side(panel, mask, in_gain, in_bias, weight):
    width = panel.shape[2]
    normed = layer_norm(panel, in_gain, in_bias).astype(jnp.bfloat16)
    flat = normed.reshape(-1, width)
    hidden = jnp.dot(flat, weight, preferred_element_type=jnp.float32)
    masked = mask.reshape(-1, 1).astype(jnp.float32)
    result = jax.nn.sigmoid(hidden[:, :width]) * hidden[:, width:] * masked
    return result.astype(jnp.bfloat16).reshape(panel.shape)


def shards(
    pair_block,
    left_panel,
    right_panel,
    mask_left,
    mask_right,
    in_gain,
    in_bias,
    w_in,
    out_gain,
    out_bias,
    w_gate_out,
    w_out,
):
    width = pair_block.shape[2]
    rows_here = pair_block.shape[0]
    cols_here = pair_block.shape[1]
    right_act = gated_side(
        right_panel, mask_right, in_gain, in_bias, w_in[:, 2 * width : 4 * width]
    )
    left_act = gated_side(left_panel, mask_left, in_gain, in_bias, w_in[:, 0 : 2 * width])
    left_all = lax.all_gather(left_act, "col", axis=1, tiled=True)
    right_all = lax.all_gather(right_act, "row", axis=1, tiled=True)
    joined = jnp.einsum("ikc,jkc->ijc", left_all, right_all, preferred_element_type=jnp.float32)
    joined_normed = layer_norm(joined, out_gain, out_bias).astype(jnp.bfloat16)
    normed_pair = layer_norm(pair_block, in_gain, in_bias).astype(jnp.bfloat16)
    gate = jnp.dot(normed_pair.reshape(-1, width), w_gate_out, preferred_element_type=jnp.float32)
    value = jnp.dot(joined_normed.reshape(-1, width), w_out, preferred_element_type=jnp.float32)
    output = (jax.nn.sigmoid(gate) * value).astype(jnp.bfloat16)
    return output.reshape(rows_here, cols_here, width)


def solution(mesh):
    placed = (
        P("row", "col", None),
        P("row", "col", None),
        P("col", "row", None),
        P("row", "col"),
        P("col", "row"),
        P(),
        P(),
        P(),
        P(),
        P(),
        P(),
        P(),
    )
    return jax.shard_map(
        shards, mesh=mesh, in_specs=placed, out_specs=P("row", "col", None), check_vma=False
    )
```

profile of v0, /device:TPU:1, one launch (start us, length us, event | category | flops | bytes accessed | tf_op | source)
XLA Modules:
  0.0 584.1 jit_solution(1377726065144957788)
XLA Ops:
  6.5 1.4 convert_reduce_fusion.2
  8.0 1.7 fusion.25
  9.6 0.7 convert_element_type.61
  10.5 1.7 fusion.28
  12.2 1.3 fusion.34
  13.6 0.3 fusion.30
  14.0 2.6 copy.18
  16.8 0.6 convert_reduce_fusion.1
  17.5 1.5 fusion.12
  19.0 1.5 fusion.15
  20.5 0.7 fusion.36
  21.2 0.7 fusion.19
  21.9 2.3 copy.16
  24.2 0.6 convert_reduce_fusion
  24.9 2.4 fusion.6
  27.2 2.5 fusion.9
  29.8 3.3 fusion.3
  33.1 173.4 %all-gather.5.cloned.1.call-done = bf16[64,512,128]{0,1,2:T(8,128)(2,1)} async-done(((bf16[64,32,128]{0,1,2:T(8,128)(2,1)}), bf16[64,512,128]{0,1,2:T(8,128)(2,1)}) %all-gather.5.cloned.1.call-update) | async-done | bytes 8388624 | tf_op jit(solution)/shard_map/all_gather | solution.py:45
  206.5 351.2 %all-gather.3.cloned.1.call-done = bf16[128,512,128]{0,1,2:T(8,128)(2,1)} async-done(((bf16[128,32,128]{0,1,2:T(8,128)(2,1)}), bf16[128,512,128]{0,1,2:T(8,128)(2,1)}) %all-gather.3.cloned.1.call-update) | async-done | bytes 16777232 | tf_op jit(solution)/shard_map/all_gather | solution.py:46
  557.7 12.9 %bitcast_reduce_fusion = (f32[64,128]{1,0:T(8,128)S(1)}, f32[128,128,64]{1,2,0:T(8,128)S(1)}) fusion(bf16[128,512,128]{0,1,2:T(8,128)(2,1)} %all-gather.3.cloned.1.call-done, bf16[64,512,128]{0,1,2:T(8,128)(2,1)} %all-gather.5.cloned.1.call-done), kind=kOutput, calls=%fused_computation.15 | convolution fusion | flops 1074782208 | bytes 29392896 | tf_op jit(solution)/shard_map/ikc,jkc->ijc/dot_general | solution.py:47
  570.7 0.5 multiply_reduce_fusion
  571.3 0.8 add_convert_fusion
  572.1 1.2 copy-done.3
  573.4 3.9 fusion.2
  (38 shorter events, 0.7 us)
Async XLA Ops:
  6.5 23.2 %copy-start = (bf16[128,128]{1,0:T(8,128)(2,1)S(1)}, bf16[128,128]{1,0:T(8,128)(2,1)}, u32[]{:S(2)}) copy-start(bf16[128,128]{1,0:T(8,128)(2,1)} %param.22) | copy-start | bytes 98308
  6.5 199.9 %all-gather.5.cloned.1.call-start = ((), (), s32[]{:S(2)}) async-start(), calls=%async_computation.1 | async-start | bytes 17825792 | tf_op jit(solution)/shard_map/all_gather | solution.py:45
  12.2 4.4 copy-start.6
  12.2 4.6 copy-start.2
  13.6 5.4 copy-start.7
  13.6 5.4 copy-start.8
  13.9 6.6 %copy-start.4 = (bf16[128,512]{1,0:T(8,128)(2,1)S(1)}, bf16[128,512]{1,0:T(8,128)(2,1)}, u32[]{:S(2)}) copy-start(bf16[128,512]{1,0:T(8,128)(2,1)} %param.19) | copy-start | bytes 393220
  16.6 541.2 %all-gather.3.cloned.1.call-start = ((), (), s32[]{:S(2)}) async-start(), calls=%async_computation | async-start | bytes 17825792 | tf_op jit(solution)/shard_map/all_gather | solution.py:46
  21.2 3.0 copy-start.1
  570.7 0.7 copy-start.9
  570.7 0.7 copy-start.10
  571.2 2.2 copy-start.3
  571.2 2.2 copy-start.5
Sparse Core Ops, SparseCore 0:
  16.7 189.7 all-gather.4
  208.3 349.4 all-gather.2
where the time goes:
time: 584 us
  waiting for transfers between devices  525 us (90%)
  matrix products  22.2 us (4%)
  other arithmetic  16.9 us (3%)
  between operations  13.7 us (2%)
  local copies, waits for them, and re-layouts  6.61 us (1%)
    all_gather x1, waiting for transfers between devices, shards(): right_all = lax.all_gather(right_act, 'row', axis=1, tiled=True)  351 us
    all_gather x1, waiting for transfers between devices, shards(): left_all = lax.all_gather(left_act, 'col', axis=1, tiled=True)  173 us
    dot_general x1, matrix products, shards(): jnp.einsum('ikc,jkc->ijc', left_all, right_all, preferred_element_type=jn...  12.9 us
  transfers between devices with their start and end apart: 2, of which 2 were waited for; matrix products, arithmetic and copies ran while one was open for 3% of the time, Pallas kernels for 0%

commit v1 on v0

v1 whole, which is shorter than its diff:
```python
import jax
import jax.numpy as jnp
from jax import lax
from jax.experimental import pallas as pl
from jax.experimental.pallas import tpu as pltpu
from jax.sharding import Mesh, PartitionSpec as P

CHIPS = ("x", "zl", "zh", "y")
EPS = 1e-05
VMEM_LIMIT = 40 * 1024 * 1024


def layer_norm(value, gain, bias):
    center = value - jnp.mean(value, axis=-1, keepdims=True)
    spread = jnp.mean(center * center, axis=-1, keepdims=True)
    return center * lax.rsqrt(spread + EPS) * gain + bias


def prologue_kernel(
    left_ref, right_ref, mask_left_ref, mask_right_ref, gain_ref, bias_ref, w_ref, out_ref, act_ref, turned_ref
):
    gain = gain_ref[...]
    bias = bias_ref[...]

    def gated(block, weight):
        rows = block.shape[0] * block.shape[1]
        value = block.astype(jnp.float32).reshape(rows, 128)
        normed = layer_norm(value, gain, bias).astype(jnp.bfloat16)
        hidden = jnp.dot(normed, weight, preferred_element_type=jnp.float32)
        return jax.nn.sigmoid(hidden[:, :128]) * hidden[:, 128:]

    def right_block(b, carry):
        block = right_ref[pl.ds(b * 16, 16)]
        act_ref[pl.ds(pl.multiple_of(b * 512, 512), 512), :] = gated(block, w_ref[:, 256:512])
        return carry

    lax.fori_loop(0, 8, right_block, 0)

    def right_turn(k, carry):
        tile = act_ref[pl.ds(k, 128, stride=32), :]
        turned_ref[pl.ds(k, 128, stride=32), :] = tile.T * mask_right_ref[pl.ds(k, 1), :].astype(jnp.float32)
        return carry

    lax.fori_loop(0, 32, right_turn, 0)

    def right_out(b, carry):
        rows = turned_ref[pl.ds(pl.multiple_of(b * 256, 256), 256), :]
        out_ref[pl.ds(b * 8, 8), 0:32, :] = rows.reshape(8, 32, 128).astype(jnp.bfloat16)
        return carry

    lax.fori_loop(0, 16, right_out, 0)

    def left_block(b, carry):
        block = left_ref[pl.ds(b * 16, 16)]
        act_ref[pl.ds(pl.multiple_of(b * 512, 512), 512), :] = gated(block, w_ref[:, 0:256])
        return carry

    lax.fori_loop(0, 4, left_block, 0)

    def left_turn(k, carry):
        low = act_ref[pl.ds(k, 64, stride=32), :]
        high = act_ref[pl.ds(k + 16, 64, stride=32), :]
        tile = jnp.concatenate([low, high], axis=0)
        turned_ref[pl.ds(k, 128, stride=16), :] = tile.T * mask_left_ref[pl.ds(k, 1), :].astype(jnp.float32)
        return carry

    lax.fori_loop(0, 16, left_turn, 0)

    def left_out(b, carry):
        rows = turned_ref[pl.ds(pl.multiple_of(b * 256, 256), 256), :]
        out_ref[pl.ds(b * 16, 16), 32:48, :] = rows.reshape(16, 16, 128).astype(jnp.bfloat16)
        return carry

    lax.fori_loop(0, 8, left_out, 0)


def join_kernel(core_ref, own_ref, other_ref, out_ref, left_ref, right_ref):
    core = core_ref[0]
    lane = lax.broadcasted_iota(jnp.int32, (16, 128), 1)
    low_half = lane < 64

    def gather(t, carry):
        for side in range(2):
            block = 2 * t + (core if side == 0 else 1 - core)
            row = pl.multiple_of((side * 8 + t) * 32, 32)
            for jb in range(8):
                right_ref[pl.ds(row, 32), jb * 128 : (jb + 1) * 128] = own_ref[block * 8 + jb, 0:32, :]
            for pair in range(8):
                if side == 0:
                    even = own_ref[pair * 16 + t, 32:48, :]
                    odd = own_ref[pair * 16 + 8 + t, 32:48, :]
                else:
                    even = other_ref[pair * 16 + t]
                    odd = other_ref[pair * 16 + 8 + t]
                even = even.astype(jnp.float32)
                odd = odd.astype(jnp.float32)
                first = jnp.where(low_half, even, pltpu.roll(odd, 64, 1))
                second = jnp.where(low_half, pltpu.roll(even, 64, 1), odd)
                both = jnp.concatenate([first, second], axis=0).astype(jnp.bfloat16)
                left_ref[pl.ds(row, 32), pair * 128 : (pair + 1) * 128] = both
        return carry

    lax.fori_loop(0, 8, gather, 0)

    def multiply(b, carry):
        lhs = left_ref[:, pl.ds(pl.multiple_of(b * 256, 256), 256)]
        total = lax.dot_general(
            lhs, right_ref[...], (((0,), (0,)), ((), ())), preferred_element_type=jnp.float32
        )
        for q in range(4):
            for jb in range(8):
                out_ref[b * 4 + q, jb] = total[q * 64 : (q + 1) * 64, jb * 128 : (jb + 1) * 128].astype(jnp.bfloat16)
        return carry

    lax.fori_loop(0, 4, multiply, 0)


def gate_kernel(pair_ref, gain_ref, bias_ref, w_ref, out_ref):
    value = pair_ref[...].astype(jnp.float32).reshape(512, 128)
    normed = layer_norm(value, gain_ref[...], bias_ref[...]).astype(jnp.bfloat16)
    gate = jnp.dot(normed, w_ref[...], preferred_element_type=jnp.float32)
    out_ref[...] = jax.nn.sigmoid(gate)


def epilogue_kernel(joined_ref, gate_ref, gain_ref, bias_ref, w_ref, out_ref, wide_ref):
    joined = joined_ref[...].astype(jnp.float32)
    mean = jnp.mean(joined, axis=0)
    center = joined - mean[None]
    spread = jnp.mean(center * center, axis=0)
    normed = center * lax.rsqrt(spread + EPS)[None]
    wide_ref[...] = normed.reshape(128 * 16, 128)
    for i in range(16):
        tile = wide_ref[pl.ds(i, 128, stride=16), :]
        tile = (tile * gain_ref[...] + bias_ref[...]).astype(jnp.bfloat16)
        value = lax.dot_general(tile, w_ref[...], (((0,), (0,)), ((), ())), preferred_element_type=jnp.float32)
        out_ref[i] = (gate_ref[i * 128 : (i + 1) * 128, :] * value).astype(jnp.bfloat16)


def shards(
    pair_block,
    left_panel,
    right_panel,
    mask_left,
    mask_right,
    in_gain,
    in_bias,
    w_in,
    out_gain,
    out_bias,
    w_gate_out,
    w_out,
):
    params = pltpu.CompilerParams(vmem_limit_bytes=VMEM_LIMIT)
    gain_row = in_gain.reshape(1, 128)
    bias_row = in_bias.reshape(1, 128)
    mask_left_turned = mask_left.T.reshape(2, 16, 64).transpose(1, 0, 2).reshape(16, 128)
    packed = pl.pallas_call(
        prologue_kernel,
        out_shape=jax.ShapeDtypeStruct((128, 48, 128), jnp.bfloat16),
        scratch_shapes=[pltpu.VMEM((4096, 128), jnp.float32), pltpu.VMEM((4096, 128), jnp.float32)],
        compiler_params=params,
        cost_estimate=pl.CostEstimate(flops=2 * 6144 * 128 * 256, bytes_accessed=3 << 20, transcendentals=6144 * 128),
    )(left_panel, right_panel, mask_left_turned, mask_right.T, gain_row, bias_row, w_in)

    mine = lax.all_to_all(packed, CHIPS, split_axis=0, concat_axis=0, tiled=True)

    gate = pl.pallas_call(
        gate_kernel,
        grid=(16,),
        in_specs=[
            pl.BlockSpec((4, 128, 128), lambda b: (b, 0, 0)),
            pl.BlockSpec((1, 128), lambda b: (0, 0)),
            pl.BlockSpec((1, 128), lambda b: (0, 0)),
            pl.BlockSpec((128, 128), lambda b: (0, 0)),
        ],
        out_specs=pl.BlockSpec((512, 128), lambda b: (b, 0)),
        out_shape=jax.ShapeDtypeStruct((8192, 128), jnp.float32),
        compiler_params=params,
        cost_estimate=pl.CostEstimate(flops=2 * 8192 * 128 * 128, bytes_accessed=6 << 20, transcendentals=8192 * 128),
    )(pair_block, gain_row, bias_row, w_gate_out)

    other_left = lax.ppermute(mine[:, 32:48, :], "core", [(0, 1), (1, 0)])
    core = lax.axis_index("core").astype(jnp.int32).reshape(1)
    joined = pl.pallas_call(
        join_kernel,
        in_specs=[
            pl.BlockSpec(memory_space=pltpu.SMEM),
            pl.BlockSpec(memory_space=pltpu.VMEM),
            pl.BlockSpec(memory_space=pltpu.VMEM),
        ],
        out_shape=jax.ShapeDtypeStruct((16, 8, 64, 128), jnp.bfloat16),
        scratch_shapes=[pltpu.VMEM((512, 1024), jnp.bfloat16), pltpu.VMEM((512, 1024), jnp.bfloat16)],
        compiler_params=params,
        cost_estimate=pl.CostEstimate(flops=2 * 1024 * 1024 * 512, bytes_accessed=4 << 20, transcendentals=0),
    )(core, mine, other_left)

    home = lax.all_to_all(joined.reshape(128, 64, 128), CHIPS, split_axis=0, concat_axis=0, tiled=True)

    return pl.pallas_call(
        epilogue_kernel,
        grid=(4,),
        in_specs=[
            pl.BlockSpec((128, 16, 128), lambda b: (0, b, 0)),
            pl.BlockSpec((2048, 128), lambda b: (b, 0)),
            pl.BlockSpec((128, 1), lambda b: (0, 0)),
            pl.BlockSpec((128, 1), lambda b: (0, 0)),
            pl.BlockSpec((128, 128), lambda b: (0, 0)),
        ],
        out_specs=pl.BlockSpec((16, 128, 128), lambda b: (b, 0, 0)),
        out_shape=jax.ShapeDtypeStruct((64, 128, 128), jnp.bfloat16),
        scratch_shapes=[pltpu.VMEM((2048, 128), jnp.float32)],
        compiler_params=params,
        cost_estimate=pl.CostEstimate(flops=2 * 8192 * 128 * 128, bytes_accessed=8 << 20, transcendentals=0),
    )(home, gate, out_gain.reshape(128, 1), out_bias.reshape(128, 1), w_out)


def solution(mesh):
    fine = Mesh(mesh.devices.reshape(4, 4, 2, 4, 2), ("x", "zl", "zh", "y", "core"))
    row = ("x", "zl")
    col = ("zh", "y", "core")
    placed = (
        P(row, col, None),
        P(row, col, None),
        P(col, row, None),
        P(row, col),
        P(col, row),
        P(),
        P(),
        P(),
        P(),
        P(),
        P(),
        P(),
    )
    return jax.shard_map(shards, mesh=fine, in_specs=placed, out_specs=P(row, col, None), check_vma=False)
```

time: 584 us -> 151 us (0.26)
  waiting for transfers between devices: 525 us -> 43.5 us
  blocking collectives: 0 us -> 56.5 us
  Pallas kernels: 0 us -> 28.3 us
  matrix products: 22.2 us -> 0 us
  other arithmetic: 16.9 us -> 0 us
  between operations: 13.7 us -> 0.12 us
  starting transfers between devices: 0.04 us -> 8.89 us
  local copies, waits for them, and re-layouts: 6.61 us -> 13.3 us
    all_gather x2 -> x0, waiting for transfers between devices: 525 us -> none  [the longest x1 351 us: shards(): right_all = lax.all_gather(right_act, 'row', axis=1, tiled=True)]
    all_to_all x0 -> x1, blocking collectives: none -> 56.5 us  [shards(): lax.all_to_all(packed, CHIPS, split_axis=0, concat_axis=0, tiled=True)]
    all_to_all x0 -> x1, waiting for transfers between devices: none -> 42 us  [shards(): lax.all_to_all(joined.reshape(128, 64, 128), CHIPS, split_axis=0, concat_...]
    pallas_call x0 -> x4, Pallas kernels: none -> 28.3 us  [the longest x1 12.7 us: shards(): pl.pallas_call(prologue_kernel, out_shape=jax.ShapeDtypeStruct((128, 48,...]
    dot_general x5 -> x0, matrix products: 22.2 us -> none  [the longest x1 12.9 us: shards(): jnp.einsum('ikc,jkc->ijc', left_all, right_all, preferred_element_type=jn...]
    unnamed x22 -> x32, local copies, waits for them, and re-layouts: 1.44 us -> 12.3 us
    reduce_sum x7 -> x0, other arithmetic: 8.58 us -> none  [the longest x4 5.96 us: layer_norm(): spread = jnp.mean(center * center, axis=-1, keepdims=True)]
    convert_element_type x8 -> x0, other arithmetic: 8.23 us -> none  [the longest x2 3.19 us: gated_side(): normed = layer_norm(panel, in_gain, in_bias).astype(jnp.bfloat16)]
  transfers between devices with their start and end apart: 2 -> 2, of which waited for: 2 -> 2; matrix products, arithmetic and copies ran while one was open for 3% -> 0% of each run, Pallas kernels for 0% -> 4%
where the time goes in v1:
time: 151 us
  blocking collectives  56.5 us (37%)
  waiting for transfers between devices  43.5 us (29%)
  Pallas kernels  28.3 us (19%)
  local copies, waits for them, and re-layouts  13.3 us (9%)
  starting transfers between devices  8.89 us (6%)
    all_to_all x1, blocking collectives, shards(): lax.all_to_all(packed, CHIPS, split_axis=0, concat_axis=0, tiled=True)  56.5 us
    all_to_all x1, waiting for transfers between devices, shards(): lax.all_to_all(joined.reshape(128, 64, 128), CHIPS, split_axis=0, concat_...  42 us
    pallas_call x1, Pallas kernels, shards(): pl.pallas_call(prologue_kernel, out_shape=jax.ShapeDtypeStruct((128, 48,...  12.7 us
    unnamed x32, local copies, waits for them, and re-layouts  12.3 us
    pallas_call x1, Pallas kernels, shards(): pl.pallas_call(epilogue_kernel, grid=(4,), in_specs=[pl.BlockSpec((128, 1...  6.88 us
    all_to_all x1, starting transfers between devices, shards(): lax.all_to_all(joined.reshape(128, 64, 128), CHIPS, split_axis=0, concat_...  6.5 us
    pallas_call x1, Pallas kernels, shards(): pl.pallas_call(gate_kernel, grid=(16,), in_specs=[pl.BlockSpec((4, 128, 1...  5.89 us
  transfers between devices with their start and end apart: 2, of which 2 were waited for; matrix products, arithmetic and copies ran while one was open for 0% of the time, Pallas kernels for 4%

profile of v1, /device:TPU:1, one launch (start us, length us, event | category | flops | bytes accessed | tf_op | source)
XLA Modules:
  0.0 150.6 jit_solution(14966298218026743416)
XLA Ops:
  0.0 0.7 copy.17
  0.7 0.1 reshape.26.mask_left_ref
  0.8 1.2 copy-done.4
  2.0 1.0 copy-done.5
  3.1 0.9 copy-done.6
  4.0 0.7 copy-done.9
  4.7 0.7 copy-done.10
  5.4 0.7 copy-done.12
  6.0 12.7 %shard_map.118 = bf16[128,48,128]{2,1,0:T(8,128)(2,1)S(1)} custom-call(bf16[64,32,128]{2,1,0:T(8,128)(2,1)S(1)} %copy-done.5, bf16[128,32,128]{2,1,0:T(8,128)(2,1)S(1)} %copy-done.4, s32[16,128]{1,0:T(8,128)S(1)} %reshape.26.mask_left_ref, s32[32,128]{1,0:T(8,128)S(1)} %bitcast.14, f32[1,128]{1,0:T(1,128)S(1)} %bitcast.15, f32[1,128]{1,0:T(1,128)S(1)} %bitcast.17, ...), custom_call_target="tpu_custom_call" | custom-call | flops 402653184 | bytes 3145728 | tf_op jit(solution)/shard_map/pallas_call | solution.py:157
  18.7 56.5 %all_to_all.10.own_ref = bf16[128,48,128]{2,1,0:T(8,128)(2,1)S(1)} all-to-all(bf16[128,48,128]{2,1,0:T(8,128)(2,1)S(1)} %shard_map.118), channel_id=1, replica_groups=mesh['x'=4,'zl'=4,'zh'=2,'y'=4,'core'=2] {'x','zl','zh','y'}, dimensions={0} | all-to-all | bytes 3145728 | tf_op jit(solution)/shard_map/all_to_all | solution.py:165
  75.2 2.4 %collective-permute-start = (bf16[128,16,128]{2,1,0:T(8,128)(2,1)S(1)}, bf16[128,16,128]{2,1,0:T(8,128)(2,1)S(1)}, u32[]{:S(2)}, u32[]{:S(2)}) collective-permute-start(bf16[128,16,128]{2,1,0:T(8,128)(2,1)S(1)} %slice.4), channel_id=1, source_target_pairs={{0,1},{1,0},{2,3},{3,2},{4,5},{5,4},{6,7},{7,6},{8,9},{9,8},{10,11... | collective-permute-start | bytes 1572872 | tf_op jit(solution)/shard_map/ppermute | solution.py:182
  77.6 1.5 %collective-permute-done.other_ref = bf16[128,16,128]{2,1,0:T(8,128)(2,1)S(1)} collective-permute-done((bf16[128,16,128]{2,1,0:T(8,128)(2,1)S(1)}, bf16[128,16,128]{2,1,0:T(8,128)(2,1)S(1)}, u32[]{:S(2)}, u32[]{:S(2)}) %collective-permute-start) | collective-permute-done | bytes 524320 | tf_op jit(solution)/shard_map/ppermute | solution.py:182
  79.1 2.8 %shard_map.119 = bf16[16,8,64,128]{3,2,1,0:T(8,128)(2,1)S(1)} custom-call(s32[1]{0:T(128)} %bitcast.core_ref, bf16[128,48,128]{2,1,0:T(8,128)(2,1)S(1)} %all_to_all.10.own_ref, bf16[128,16,128]{2,1,0:T(8,128)(2,1)S(1)} %collective-permute-done.other_ref), custom_call_target="tpu_custom_call" | custom-call | flops 1073741824 | bytes 4194304 | tf_op jit(solution)/shard_map/pallas_call | solution.py:184
  82.0 0.0 copy-start.2
  82.0 1.3 copy-done.2
  83.3 6.5 %all-to-all-start.1 = ((bf16[128,64,128]{2,1,0:T(8,128)(2,1)}), bf16[128,64,128]{2,1,0:T(8,128)(2,1)S(1)}, u32[]{:S(2)}, u32[]{:S(2)}) async-start(bf16[128,64,128]{2,1,0:T(8,128)(2,1)} %bitcast.13), calls=%async_computation.1 | async-start | bytes 4194304 | tf_op jit(solution)/shard_map/all_to_all | solution.py:197
  89.8 0.1 copy.14.gain_ref
  90.0 0.1 copy.15.bias_ref
  90.1 1.6 %copy-done.3 = bf16[64,128,128]{2,1,0:T(8,128)(2,1)S(1)} copy-done((bf16[64,128,128]{2,1,0:T(8,128)(2,1)S(1)}, bf16[64,128,128]{2,1,0:T(8,128)(2,1)}, u32[]{:S(2)}) %copy-start.3) | copy-done | bytes 2097176
  91.7 5.9 %shard_map.120.gate_ref = f32[8192,128]{1,0:T(8,128)S(1)} custom-call(bf16[64,128,128]{2,1,0:T(8,128)(2,1)S(1)} %copy-done.3, f32[1,128]{1,0:T(1,128)S(1)} %bitcast.16, f32[1,128]{1,0:T(1,128)S(1)} %bitcast.18, bf16[128,128]{1,0:T(8,128)(2,1)S(1)} %copy-done.7), custom_call_target="tpu_custom_call" | custom-call | flops 268435456 | bytes 6291456 | tf_op jit(solution)/shard_map/pallas_call | solution.py:167
  97.6 1.9 %copy-done = f32[8192,128]{1,0:T(8,128)} copy-done((f32[8192,128]{1,0:T(8,128)}, f32[8192,128]{1,0:T(8,128)S(1)}, u32[]{:S(2)}) %copy-start) | copy-done | bytes 4194328
  99.5 42.0 %all-to-all-done.1.joined_ref = bf16[128,64,128]{2,1,0:T(8,128)(2,1)S(1)} async-done(((bf16[128,64,128]{2,1,0:T(8,128)(2,1)}), bf16[128,64,128]{2,1,0:T(8,128)(2,1)S(1)}, u32[]{:S(2)}, u32[]{:S(2)}) %all-to-all-start.1) | async-done | bytes 2097184 | tf_op jit(solution)/shard_map/all_to_all | solution.py:197
  141.5 2.2 %copy-done.1 = f32[8192,128]{1,0:T(8,128)S(1)} copy-done((f32[8192,128]{1,0:T(8,128)S(1)}, f32[8192,128]{1,0:T(8,128)}, u32[]{:S(2)}) %copy-start.1) | copy-done | bytes 4194328
  143.7 6.9 %shard_map.121 = bf16[64,128,128]{2,1,0:T(8,128)(2,1)} custom-call(bf16[128,64,128]{2,1,0:T(8,128)(2,1)S(1)} %all-to-all-done.1.joined_ref, f32[8192,128]{1,0:T(8,128)S(1)} %copy-done.1, f32[128,1]{1,0:T(8,128)S(1)} %copy.14.gain_ref, f32[128,1]{1,0:T(8,128)S(1)} %copy.15.bias_ref, bf16[128,128]{1,0:T(8,128)(2,1)S(1)} %copy-done.8), custom_call_target="tpu_custom_call" | custom-call | flops 268435456 | bytes 8388608 | tf_op jit(solution)/shard_map/pallas_call | solution.py:199
  (22 shorter events, 0.1 us)
Async XLA Ops:
  0.8 1.2 copy-start.4
  2.0 1.0 copy-start.5
  3.1 0.9 copy-start.6
  4.0 0.7 copy-start.9
  4.7 0.7 copy-start.10
  5.4 0.7 copy-start.12
  75.2 3.9 %collective-permute-start = (bf16[128,16,128]{2,1,0:T(8,128)(2,1)S(1)}, bf16[128,16,128]{2,1,0:T(8,128)(2,1)S(1)}, u32[]{:S(2)}, u32[]{:S(2)}) collective-permute-start(bf16[128,16,128]{2,1,0:T(8,128)(2,1)S(1)} %slice.4), channel_id=1, source_target_pairs={{0,1},{1,0},{2,3},{3,2},{4,5},{5,4},{6,7},{7,6},{8,9},{9,8},{10,11... | collective-permute-start | bytes 1572872 | tf_op jit(solution)/shard_map/ppermute | solution.py:182
  82.0 1.3 copy-start.2
  83.3 6.5 %copy-start.14 = (f32[128]{0:T(128)S(1)}, f32[128]{0:T(128)}, u32[]{:S(2)}) copy-start(f32[128]{0:T(128)} %param.20) | copy-start | bytes 1540
  83.3 6.7 %copy-start.15 = (f32[128]{0:T(128)S(1)}, f32[128]{0:T(128)}, u32[]{:S(2)}) copy-start(f32[128]{0:T(128)} %param.21) | copy-start | bytes 1540
  83.3 6.8 %copy-start.7 = (bf16[128,128]{1,0:T(8,128)(2,1)S(1)}, bf16[128,128]{1,0:T(8,128)(2,1)}, u32[]{:S(2)}) copy-start(bf16[128,128]{1,0:T(8,128)(2,1)} %w_ref.4) | copy-start | bytes 98308
  83.3 6.8 %copy-start.11 = (f32[128]{0:T(128)S(1)}, f32[128]{0:T(128)}, u32[]{:S(2)}) copy-start(f32[128]{0:T(128)} %param.17) | copy-start | bytes 1540
  83.3 6.8 %copy-start.13 = (f32[128]{0:T(128)S(1)}, f32[128]{0:T(128)}, u32[]{:S(2)}) copy-start(f32[128]{0:T(128)} %param.18) | copy-start | bytes 1540
  83.3 58.2 %all-to-all-start.1 = ((bf16[128,64,128]{2,1,0:T(8,128)(2,1)}), bf16[128,64,128]{2,1,0:T(8,128)(2,1)S(1)}, u32[]{:S(2)}, u32[]{:S(2)}) async-start(bf16[128,64,128]{2,1,0:T(8,128)(2,1)} %bitcast.13), calls=%async_computation.1 | async-start | bytes 4194304 | tf_op jit(solution)/shard_map/all_to_all | solution.py:197
  90.1 1.6 %copy-start.3 = (bf16[64,128,128]{2,1,0:T(8,128)(2,1)S(1)}, bf16[64,128,128]{2,1,0:T(8,128)(2,1)}, u32[]{:S(2)}) copy-start(bf16[64,128,128]{2,1,0:T(8,128)(2,1)} %pair_ref.1) | copy-start | bytes 6291460
  91.7 49.8 %copy-start.8 = (bf16[128,128]{1,0:T(8,128)(2,1)S(1)}, bf16[128,128]{1,0:T(8,128)(2,1)}, u32[]{:S(2)}) copy-start(bf16[128,128]{1,0:T(8,128)(2,1)} %w_ref.5) | copy-start | bytes 98308
  97.6 2.0 %copy-start = (f32[8192,128]{1,0:T(8,128)}, f32[8192,128]{1,0:T(8,128)S(1)}, u32[]{:S(2)}) copy-start(f32[8192,128]{1,0:T(8,128)S(1)} %shard_map.120.gate_ref) | copy-start | bytes 12582916
  141.5 2.2 %copy-start.1 = (f32[8192,128]{1,0:T(8,128)S(1)}, f32[8192,128]{1,0:T(8,128)}, u32[]{:S(2)}) copy-start(f32[8192,128]{1,0:T(8,128)} %copy-done) | copy-start | bytes 12582916

commit v2 on v1

v2 whole, which is shorter than its diff:
```python
import functools

import jax
import jax.numpy as jnp
from jax import lax
from jax.experimental import pallas as pl
from jax.experimental.pallas import tpu as pltpu
from jax.sharding import Mesh, PartitionSpec as P

CHIPS = ("x", "zl", "zh", "y")
EPS = 1e-05
VMEM_LIMIT = 40 * 1024 * 1024
PITCH = 40
HBM = pltpu.HBM


def layer_norm(value, gain, bias):
    center = value - jnp.mean(value, axis=-1, keepdims=True)
    spread = jnp.mean(center * center, axis=-1, keepdims=True)
    return center * lax.rsqrt(spread + EPS) * gain + bias


def prologue_kernel(
    left_hbm,
    right_hbm,
    mask_left_hbm,
    mask_right_hbm,
    gain_hbm,
    bias_hbm,
    w_hbm,
    out_ref,
    left_ref,
    right_ref,
    mask_left_ref,
    mask_right_ref,
    gain_ref,
    bias_ref,
    w_ref,
    act_ref,
    turned_ref,
    mask_ref,
    sems,
):
    right_copies = [
        pltpu.make_async_copy(right_hbm.at[pl.ds(b * 64, 64)], right_ref.at[pl.ds(b * 64, 64)], sems.at[b])
        for b in range(2)
    ]
    small_copies = [
        pltpu.make_async_copy(gain_hbm, gain_ref, sems.at[2]),
        pltpu.make_async_copy(bias_hbm, bias_ref, sems.at[3]),
        pltpu.make_async_copy(w_hbm, w_ref, sems.at[4]),
        pltpu.make_async_copy(mask_right_hbm, mask_right_ref, sems.at[5]),
        pltpu.make_async_copy(mask_left_hbm, mask_left_ref, sems.at[6]),
    ]
    left_copy = pltpu.make_async_copy(left_hbm, left_ref, sems.at[7])
    right_copies[0].start()
    for copy in small_copies:
        copy.start()
    right_copies[1].start()
    left_copy.start()
    ones = jnp.full((128, 128), 1 / 128, jnp.bfloat16)

    def norm_block(source, b, carry):
        flat = source[pl.ds(b * 16, 16)].reshape(512, 128)
        mean = jnp.dot(flat, ones, preferred_element_type=jnp.float32)
        center = flat.astype(jnp.float32) - mean
        spread = jnp.mean(center * center, axis=-1, keepdims=True)
        normed = center * lax.rsqrt(spread + EPS) * gain_ref[...] + bias_ref[...]
        for token in range(16):
            row = pl.multiple_of((b * 16 + token) * PITCH, 8)
            act_ref[pl.ds(row, 32), :] = normed[token * 32 : (token + 1) * 32]
        return carry

    def gated(tile, weight, mask):
        hidden = lax.dot_general(
            weight, tile.astype(jnp.bfloat16), (((0,), (1,)), ((), ())), preferred_element_type=jnp.float32
        )
        return (jnp.tanh(hidden[:128] * 0.5) * 0.5 + 0.5) * hidden[128:] * mask

    for copy in small_copies[:4]:
        copy.wait()
    for half in range(2):
        right_copies[half].wait()
        lax.fori_loop(half * 4, half * 4 + 4, functools.partial(norm_block, right_ref), 0, unroll=4)
    right_weight = w_ref[:, 256:512]

    def right_turn(k, carry):
        tile = act_ref[pl.ds(k, 128, stride=PITCH), :]
        mask = mask_right_ref[pl.ds(k, 1), :].astype(jnp.float32)
        turned_ref[pl.ds(k, 128, stride=PITCH), :] = gated(tile, right_weight, mask)
        return carry

    lax.fori_loop(0, 32, right_turn, 0, unroll=16)

    def right_out(b, carry):
        for q in range(8):
            row = pl.multiple_of((b * 8 + q) * PITCH, 8)
            out_ref[b * 8 + q, 0:32, :] = turned_ref[pl.ds(row, 32), :].astype(jnp.bfloat16)
        return carry

    lax.fori_loop(0, 16, right_out, 0, unroll=4)

    small_copies[4].wait()
    mask_left = mask_left_ref[...].astype(jnp.float32)
    mask_ref[...] = jnp.concatenate([mask_left[0:16], mask_left[16:32]], axis=1)
    left_copy.wait()
    lax.fori_loop(0, 4, functools.partial(norm_block, left_ref), 0, unroll=4)
    left_weight = w_ref[:, 0:256]

    def left_turn(k, carry):
        low = act_ref[pl.ds(k, 64, stride=PITCH), :]
        high = act_ref[pl.ds(k + 16, 64, stride=PITCH), :]
        tile = jnp.concatenate([low, high], axis=0)
        turned_ref[pl.ds(k, 128, stride=24), :] = gated(tile, left_weight, mask_ref[pl.ds(k, 1), :])
        return carry

    lax.fori_loop(0, 16, left_turn, 0, unroll=16)

    def left_out(b, carry):
        for q in range(8):
            row = pl.multiple_of((b * 8 + q) * 24, 8)
            out_ref[b * 8 + q, 32:48, :] = turned_ref[pl.ds(row, 16), :].astype(jnp.bfloat16)
        return carry

    lax.fori_loop(0, 16, left_out, 0, unroll=4)


def join_kernel(core_ref, own_ref, other_ref, out_ref, left_ref, right_ref):
    core = core_ref[0]
    lane = lax.broadcasted_iota(jnp.int32, (16, 128), 1)
    low_half = lane < 64

    def gather(t, carry):
        for side in range(2):
            block = 2 * t + (core if side == 0 else 1 - core)
            row = pl.multiple_of((side * 8 + t) * 32, 32)
            for jb in range(8):
                right_ref[pl.ds(row, 32), jb * 128 : (jb + 1) * 128] = own_ref[block * 8 + jb, 0:32, :]
            for pair in range(8):
                if side == 0:
                    even = own_ref[pair * 16 + t, 32:48, :]
                    odd = own_ref[pair * 16 + 8 + t, 32:48, :]
                else:
                    even = other_ref[pair * 16 + t]
                    odd = other_ref[pair * 16 + 8 + t]
                even = even.astype(jnp.float32)
                odd = odd.astype(jnp.float32)
                first = jnp.where(low_half, even, pltpu.roll(odd, 64, 1))
                second = jnp.where(low_half, pltpu.roll(even, 64, 1), odd)
                both = jnp.concatenate([first, second], axis=0).astype(jnp.bfloat16)
                left_ref[pl.ds(row, 32), pair * 128 : (pair + 1) * 128] = both
        return carry

    @pl.when(pl.program_id(0) == 0)
    def _():
        lax.fori_loop(0, 8, gather, 0, unroll=2)

    column = pl.multiple_of(pl.program_id(0) * 256, 256)
    total = lax.dot_general(
        left_ref[:, pl.ds(column, 256)], right_ref[...], (((0,), (0,)), ((), ())), preferred_element_type=jnp.float32
    )
    for q in range(4):
        for jb in range(8):
            out_ref[q * 8 + jb] = total[q * 64 : (q + 1) * 64, jb * 128 : (jb + 1) * 128].astype(jnp.bfloat16)


def gate_kernel(pair_ref, gain_ref, bias_ref, w_ref, out_ref):
    value = pair_ref[...].astype(jnp.float32).reshape(512, 128)
    normed = layer_norm(value, gain_ref[...], bias_ref[...]).astype(jnp.bfloat16)
    gate = jnp.dot(normed, w_ref[...], preferred_element_type=jnp.float32)
    out_ref[...] = jax.nn.sigmoid(gate)


def epilogue_kernel(joined_ref, gate_ref, gain_ref, bias_ref, w_ref, out_ref, wide_ref):
    gain = jnp.broadcast_to(gain_ref[...], (128, 128))
    bias = jnp.broadcast_to(bias_ref[...], (128, 128))
    zero = jnp.zeros((16, 128), jnp.float32)

    def total_of(c, total):
        value = joined_ref[c].astype(jnp.float32)
        wide_ref[pl.ds(pl.multiple_of(c * 24, 8), 16), :] = value
        return total + value

    mean = lax.fori_loop(0, 128, total_of, zero, unroll=16) * (1 / 128)

    def squares_of(c, total):
        center = wide_ref[pl.ds(pl.multiple_of(c * 24, 8), 16), :] - mean
        return total + center * center

    scale = lax.rsqrt(lax.fori_loop(0, 128, squares_of, zero, unroll=16) * (1 / 128) + EPS)
    for i in range(16):
        tile = wide_ref[pl.ds(i, 128, stride=24), :]
        tile = ((tile - mean[i : i + 1]) * scale[i : i + 1] * gain + bias).astype(jnp.bfloat16)
        value = lax.dot_general(tile, w_ref[...], (((0,), (0,)), ((), ())), preferred_element_type=jnp.float32)
        out_ref[i] = (gate_ref[i * 128 : (i + 1) * 128, :] * value).astype(jnp.bfloat16)


def shards(
    pair_block,
    left_panel,
    right_panel,
    mask_left,
    mask_right,
    in_gain,
    in_bias,
    w_in,
    out_gain,
    out_bias,
    w_gate_out,
    w_out,
):
    params = pltpu.CompilerParams(vmem_limit_bytes=VMEM_LIMIT)
    gain_row = in_gain.reshape(1, 128)
    bias_row = in_bias.reshape(1, 128)
    hbm = pl.BlockSpec(memory_space=HBM)
    packed = pl.pallas_call(
        prologue_kernel,
        in_specs=[hbm] * 7,
        out_shape=jax.ShapeDtypeStruct((128, 48, 128), jnp.bfloat16),
        scratch_shapes=[
            pltpu.VMEM((64, 32, 128), jnp.bfloat16),
            pltpu.VMEM((128, 32, 128), jnp.bfloat16),
            pltpu.VMEM((32, 64), jnp.int32),
            pltpu.VMEM((32, 128), jnp.int32),
            pltpu.VMEM((1, 128), jnp.float32),
            pltpu.VMEM((1, 128), jnp.float32),
            pltpu.VMEM((128, 512), jnp.bfloat16),
            pltpu.VMEM((128 * PITCH, 128), jnp.float32),
            pltpu.VMEM((128 * PITCH, 128), jnp.float32),
            pltpu.VMEM((16, 128), jnp.float32),
            pltpu.SemaphoreType.DMA((8,)),
        ],
        compiler_params=params,
        cost_estimate=pl.CostEstimate(flops=2 * 6144 * 128 * 256, bytes_accessed=3 << 20, transcendentals=6144 * 128),
    )(*[pltpu.with_memory_space_constraint(item, HBM) for item in (left_panel, right_panel, mask_left.T, mask_right.T, gain_row, bias_row, w_in)])

    mine = lax.all_to_all(packed, CHIPS, split_axis=0, concat_axis=0, tiled=True)

    gate = pl.pallas_call(
        gate_kernel,
        grid=(16,),
        in_specs=[
            pl.BlockSpec((4, 128, 128), lambda b: (b, 0, 0)),
            pl.BlockSpec((1, 128), lambda b: (0, 0)),
            pl.BlockSpec((1, 128), lambda b: (0, 0)),
            pl.BlockSpec((128, 128), lambda b: (0, 0)),
        ],
        out_specs=pl.BlockSpec((512, 128), lambda b: (b, 0)),
        out_shape=HBM((8192, 128), jnp.float32),
        compiler_params=params,
        cost_estimate=pl.CostEstimate(flops=2 * 8192 * 128 * 128, bytes_accessed=6 << 20, transcendentals=8192 * 128),
    )(pair_block, gain_row, bias_row, w_gate_out)

    other_left = lax.ppermute(mine[:, 32:48, :], "core", [(0, 1), (1, 0)])
    core = lax.axis_index("core").astype(jnp.int32).reshape(1)
    joined = pl.pallas_call(
        join_kernel,
        grid=(4,),
        in_specs=[
            pl.BlockSpec(memory_space=pltpu.SMEM),
            pl.BlockSpec(memory_space=pltpu.VMEM),
            pl.BlockSpec(memory_space=pltpu.VMEM),
        ],
        out_specs=pl.BlockSpec((32, 64, 128), lambda b: (b, 0, 0)),
        out_shape=HBM((128, 64, 128), jnp.bfloat16),
        scratch_shapes=[pltpu.VMEM((512, 1024), jnp.bfloat16), pltpu.VMEM((512, 1024), jnp.bfloat16)],
        compiler_params=params,
        cost_estimate=pl.CostEstimate(flops=2 * 1024 * 1024 * 512, bytes_accessed=4 << 20, transcendentals=0),
    )(core, mine, other_left)

    home = lax.all_to_all(joined, CHIPS, split_axis=0, concat_axis=0, tiled=True)

    return pl.pallas_call(
        epilogue_kernel,
        grid=(4,),
        in_specs=[
            pl.BlockSpec((128, 16, 128), lambda b: (0, b, 0)),
            pl.BlockSpec((2048, 128), lambda b: (b, 0)),
            pl.BlockSpec((128, 1), lambda b: (0, 0)),
            pl.BlockSpec((128, 1), lambda b: (0, 0)),
            pl.BlockSpec((128, 128), lambda b: (0, 0)),
        ],
        out_specs=pl.BlockSpec((16, 128, 128), lambda b: (b, 0, 0)),
        out_shape=jax.ShapeDtypeStruct((64, 128, 128), jnp.bfloat16),
        scratch_shapes=[pltpu.VMEM((128 * 24, 128), jnp.float32)],
        compiler_params=params,
        cost_estimate=pl.CostEstimate(flops=2 * 8192 * 128 * 128, bytes_accessed=8 << 20, transcendentals=0),
    )(home, pltpu.with_memory_space_constraint(gate, HBM), out_gain.reshape(128, 1), out_bias.reshape(128, 1), w_out)


def solution(mesh):
    fine = Mesh(mesh.devices.reshape(4, 4, 2, 4, 2), ("x", "zl", "zh", "y", "core"))
    row = ("x", "zl")
    col = ("zh", "y", "core")
    placed = (
        P(row, col, None),
        P(row, col, None),
        P(col, row, None),
        P(row, col),
        P(col, row),
        P(),
        P(),
        P(),
        P(),
        P(),
        P(),
        P(),
    )
    return jax.shard_map(shards, mesh=fine, in_specs=placed, out_specs=P(row, col, None), check_vma=False)
```

time: 151 us -> 134 us (0.89)
  local copies, waits for them, and re-layouts: 13.3 us -> 1.87 us
  Pallas kernels: 28.3 us -> 23.4 us
    unnamed x32 -> x14, local copies, waits for them, and re-layouts: 12.3 us -> 1.61 us
    pallas_call x2, Pallas kernels: 15.5 us -> 8.38 us  [the longest x1 4.63 us: shards(): pl.pallas_call(prologue_kernel, in_specs=[hbm] * 7, out_shape=jax.ShapeDt...]
    pallas_call x1, Pallas kernels: 5.89 us -> 8.87 us  [shards(): pl.pallas_call(gate_kernel, grid=(16,), in_specs=[pl.BlockSpec((4, 128, 1...]
  transfers between devices with their start and end apart: 2 -> 2, of which waited for: 2 -> 2; matrix products, arithmetic and copies ran while one was open for 0% -> 0% of each run, Pallas kernels for 4% -> 7%
where the time goes in v2:
time: 134 us; the launch traced here: 133 us
  blocking collectives  56.5 us (42%)
  waiting for transfers between devices  42.5 us (32%)
  Pallas kernels  23.4 us (17%)
  starting transfers between devices  8.89 us (7%)
  local copies, waits for them, and re-layouts  1.87 us (1%)
    all_to_all x1, blocking collectives, shards(): lax.all_to_all(packed, CHIPS, split_axis=0, concat_axis=0, tiled=True)  56.5 us
    all_to_all x1, waiting for transfers between devices, shards(): lax.all_to_all(joined, CHIPS, split_axis=0, concat_axis=0, tiled=True)  41 us
    pallas_call x1, Pallas kernels, shards(): pl.pallas_call(gate_kernel, grid=(16,), in_specs=[pl.BlockSpec((4, 128, 1...  8.87 us
    all_to_all x1, starting transfers between devices, shards(): lax.all_to_all(joined, CHIPS, split_axis=0, concat_axis=0, tiled=True)  6.5 us
    pallas_call x1, Pallas kernels, shards(): pl.pallas_call(epilogue_kernel, grid=(4,), in_specs=[pl.BlockSpec((128, 1...  6.18 us
    pallas_call x1, Pallas kernels, shards(): pl.pallas_call(prologue_kernel, in_specs=[hbm] * 7, out_shape=jax.ShapeDt...  4.63 us
    pallas_call x1, Pallas kernels, shards(): pl.pallas_call(join_kernel, grid=(4,), in_specs=[pl.BlockSpec(memory_spac...  3.75 us
  transfers between devices with their start and end apart: 2, of which 2 were waited for; matrix products, arithmetic and copies ran while one was open for 0% of the time, Pallas kernels for 7%

profile of v2, /device:TPU:1, one launch (start us, length us, event | category | flops | bytes accessed | tf_op | source)
XLA Modules:
  0.0 133.2 jit_solution(16716707005088326171)
XLA Ops:
  0.0 4.6 %shard_map.118 = bf16[128,48,128]{2,1,0:T(8,128)(2,1)S(1)} custom-call(bf16[64,32,128]{2,1,0:T(8,128)(2,1)} %left_hbm.1, bf16[128,32,128]{2,1,0:T(8,128)(2,1)} %right_hbm.1, s32[32,64]{1,0:T(8,128)} %bitcast.11, s32[32,128]{1,0:T(8,128)} %bitcast.12, f32[1,128]{1,0:T(1,128)} %bitcast.7, f32[1,128]{1,0:T(1,128)} %bitcast.9, bf16[128,512]{1,0:T(8,128)(2,1)} %w_hbm.1), custom_call_target="tpu_custom_call" | custom-call | flops 402653184 | bytes 3145728 | tf_op jit(solution)/shard_map/pallas_call | solution.py:216
  4.6 56.5 %all_to_all.10.own_ref = bf16[128,48,128]{2,1,0:T(8,128)(2,1)S(1)} all-to-all(bf16[128,48,128]{2,1,0:T(8,128)(2,1)S(1)} %shard_map.118), channel_id=1, replica_groups=mesh['x'=4,'zl'=4,'zh'=2,'y'=4,'core'=2] {'x','zl','zh','y'}, dimensions={0} | all-to-all | bytes 3145728 | tf_op jit(solution)/shard_map/all_to_all | solution.py:237
  61.1 2.4 %collective-permute-start = (bf16[128,16,128]{2,1,0:T(8,128)(2,1)S(1)}, bf16[128,16,128]{2,1,0:T(8,128)(2,1)S(1)}, u32[]{:S(2)}, u32[]{:S(2)}) collective-permute-start(bf16[128,16,128]{2,1,0:T(8,128)(2,1)S(1)} %slice.4), channel_id=1, source_target_pairs={{0,1},{1,0},{2,3},{3,2},{4,5},{5,4},{6,7},{7,6},{8,9},{9,8},{10,11... | collective-permute-start | bytes 1572872 | tf_op jit(solution)/shard_map/ppermute | solution.py:254
  63.5 1.5 %collective-permute-done.other_ref = bf16[128,16,128]{2,1,0:T(8,128)(2,1)S(1)} collective-permute-done((bf16[128,16,128]{2,1,0:T(8,128)(2,1)S(1)}, bf16[128,16,128]{2,1,0:T(8,128)(2,1)S(1)}, u32[]{:S(2)}, u32[]{:S(2)}) %collective-permute-start) | collective-permute-done | bytes 524320 | tf_op jit(solution)/shard_map/ppermute | solution.py:254
  65.1 3.8 %shard_map.119 = bf16[128,64,128]{2,1,0:T(8,128)(2,1)} custom-call(s32[1]{0:T(128)} %bitcast.core_ref, bf16[128,48,128]{2,1,0:T(8,128)(2,1)S(1)} %all_to_all.10.own_ref, bf16[128,16,128]{2,1,0:T(8,128)(2,1)S(1)} %collective-permute-done.other_ref), custom_call_target="tpu_custom_call" | custom-call | flops 1073741824 | bytes 4194304 | tf_op jit(solution)/shard_map/pallas_call | solution.py:256
  68.8 0.0 copy-start.5
  68.8 0.0 copy-start.6
  68.8 0.0 copy-start.1
  68.8 0.0 copy-start.3
  68.8 0.0 copy-start.4
  68.8 6.5 %all-to-all-start.1 = ((bf16[128,64,128]{2,1,0:T(8,128)(2,1)}), bf16[128,64,128]{2,1,0:T(8,128)(2,1)S(1)}, u32[]{:S(2)}, u32[]{:S(2)}) async-start(bf16[128,64,128]{2,1,0:T(8,128)(2,1)} %shard_map.119), calls=%async_computation.1 | async-start | bytes 4194304 | tf_op jit(solution)/shard_map/all_to_all | solution.py:271
  75.4 0.0 copy-done.5
  75.4 0.1 copy.13.gain_ref
  75.5 0.0 copy-done.6
  75.5 0.1 copy.14.bias_ref
  75.6 0.0 copy-done.1
  75.6 0.0 copy-done.3
  75.6 0.0 copy-done.4
  75.6 0.0 copy-start
  75.6 1.6 %copy-done = bf16[64,128,128]{2,1,0:T(8,128)(2,1)S(1)} copy-done((bf16[64,128,128]{2,1,0:T(8,128)(2,1)S(1)}, bf16[64,128,128]{2,1,0:T(8,128)(2,1)}, u32[]{:S(2)}) %copy-start) | copy-done | bytes 2097176
  77.2 8.9 %shard_map.120.gate_ref = f32[8192,128]{1,0:T(8,128)} custom-call(bf16[64,128,128]{2,1,0:T(8,128)(2,1)S(1)} %copy-done, f32[1,128]{1,0:T(1,128)S(1)} %bitcast.8, f32[1,128]{1,0:T(1,128)S(1)} %bitcast.10, bf16[128,128]{1,0:T(8,128)(2,1)S(1)} %copy-done.1), custom_call_target="tpu_custom_call" | custom-call | flops 268435456 | bytes 6291456 | tf_op jit(solution)/shard_map/pallas_call | solution.py:239
  86.1 41.0 %all-to-all-done.1.joined_ref = bf16[128,64,128]{2,1,0:T(8,128)(2,1)S(1)} async-done(((bf16[128,64,128]{2,1,0:T(8,128)(2,1)}), bf16[128,64,128]{2,1,0:T(8,128)(2,1)S(1)}, u32[]{:S(2)}, u32[]{:S(2)}) %all-to-all-start.1) | async-done | bytes 2097184 | tf_op jit(solution)/shard_map/all_to_all | solution.py:271
  127.1 0.0 copy-done.2
  127.1 6.2 %shard_map.121 = bf16[64,128,128]{2,1,0:T(8,128)(2,1)} custom-call(bf16[128,64,128]{2,1,0:T(8,128)(2,1)S(1)} %all-to-all-done.1.joined_ref, f32[8192,128]{1,0:T(8,128)} %shard_map.120.gate_ref, f32[128,1]{1,0:T(8,128)S(1)} %copy.13.gain_ref, f32[128,1]{1,0:T(8,128)S(1)} %copy.14.bias_ref, bf16[128,128]{1,0:T(8,128)(2,1)S(1)} %copy-done.2), custom_call_target="tpu_custom_call" | custom-call | flops 268435456 | bytes 8388608 | tf_op jit(solution)/shard_map/pallas_call | solution.py:273
  (2 shorter events, 0.0 us)
Async XLA Ops:
  61.1 3.9 %collective-permute-start = (bf16[128,16,128]{2,1,0:T(8,128)(2,1)S(1)}, bf16[128,16,128]{2,1,0:T(8,128)(2,1)S(1)}, u32[]{:S(2)}, u32[]{:S(2)}) collective-permute-start(bf16[128,16,128]{2,1,0:T(8,128)(2,1)S(1)} %slice.4), channel_id=1, source_target_pairs={{0,1},{1,0},{2,3},{3,2},{4,5},{5,4},{6,7},{7,6},{8,9},{9,8},{10,11... | collective-permute-start | bytes 1572872 | tf_op jit(solution)/shard_map/ppermute | solution.py:254
  68.8 6.5 %copy-start.5 = (f32[128]{0:T(128)S(1)}, f32[128]{0:T(128)}, u32[]{:S(2)}) copy-start(f32[128]{0:T(128)} %param.20) | copy-start | bytes 1540
  68.8 6.7 %copy-start.6 = (f32[128]{0:T(128)S(1)}, f32[128]{0:T(128)}, u32[]{:S(2)}) copy-start(f32[128]{0:T(128)} %param.21) | copy-start | bytes 1540
  68.8 6.8 %copy-start.1 = (bf16[128,128]{1,0:T(8,128)(2,1)S(1)}, bf16[128,128]{1,0:T(8,128)(2,1)}, u32[]{:S(2)}) copy-start(bf16[128,128]{1,0:T(8,128)(2,1)} %w_ref.2) | copy-start | bytes 98308
  68.8 6.8 %copy-start.3 = (f32[128]{0:T(128)S(1)}, f32[128]{0:T(128)}, u32[]{:S(2)}) copy-start(f32[128]{0:T(128)} %param.17) | copy-start | bytes 1540
  68.8 6.8 %copy-start.4 = (f32[128]{0:T(128)S(1)}, f32[128]{0:T(128)}, u32[]{:S(2)}) copy-start(f32[128]{0:T(128)} %param.18) | copy-start | bytes 1540
  68.8 58.2 %all-to-all-start.1 = ((bf16[128,64,128]{2,1,0:T(8,128)(2,1)}), bf16[128,64,128]{2,1,0:T(8,128)(2,1)S(1)}, u32[]{:S(2)}, u32[]{:S(2)}) async-start(bf16[128,64,128]{2,1,0:T(8,128)(2,1)} %shard_map.119), calls=%async_computation.1 | async-start | bytes 4194304 | tf_op jit(solution)/shard_map/all_to_all | solution.py:271
  75.6 1.6 %copy-start = (bf16[64,128,128]{2,1,0:T(8,128)(2,1)S(1)}, bf16[64,128,128]{2,1,0:T(8,128)(2,1)}, u32[]{:S(2)}) copy-start(bf16[64,128,128]{2,1,0:T(8,128)(2,1)} %pair_ref.1) | copy-start | bytes 6291460
  77.2 49.8 %copy-start.2 = (bf16[128,128]{1,0:T(8,128)(2,1)S(1)}, bf16[128,128]{1,0:T(8,128)(2,1)}, u32[]{:S(2)}) copy-start(bf16[128,128]{1,0:T(8,128)(2,1)} %w_ref.3) | copy-start | bytes 98308

commit v3 on v2

--- a/solution.py
+++ b/solution.py
@@ -155,11 +155,11 @@
     def _():
         lax.fori_loop(0, 8, gather, 0, unroll=2)
 
-    column = pl.multiple_of(pl.program_id(0) * 256, 256)
+    column = pl.multiple_of(pl.program_id(0) * 512, 512)
     total = lax.dot_general(
-        left_ref[:, pl.ds(column, 256)], right_ref[...], (((0,), (0,)), ((), ())), preferred_element_type=jnp.float32
+        left_ref[:, pl.ds(column, 512)], right_ref[...], (((0,), (0,)), ((), ())), preferred_element_type=jnp.float32
     )
-    for q in range(4):
+    for q in range(8):
         for jb in range(8):
             out_ref[q * 8 + jb] = total[q * 64 : (q + 1) * 64, jb * 128 : (jb + 1) * 128].astype(jnp.bfloat16)
 
@@ -171,28 +171,38 @@
     out_ref[...] = jax.nn.sigmoid(gate)
 
 
-def epilogue_kernel(joined_ref, gate_ref, gain_ref, bias_ref, w_ref, out_ref, wide_ref):
+def epilogue_kernel(joined_ref, gate_hbm, gain_ref, bias_ref, w_ref, out_ref, wide_ref, gate_ref, sems):
+    step = pl.program_id(0)
+
+    def gate_copy(part):
+        rows = pl.ds(pl.multiple_of(part * 2048, 2048), 2048)
+        return pltpu.make_async_copy(gate_hbm.at[rows], gate_ref.at[rows], sems.at[part])
+
+    @pl.when(step == 0)
+    def _():
+        for part in range(4):
+            gate_copy(part).start()
+
     gain = jnp.broadcast_to(gain_ref[...], (128, 128))
     bias = jnp.broadcast_to(bias_ref[...], (128, 128))
     zero = jnp.zeros((16, 128), jnp.float32)
-
-    def total_of(c, total):
-        value = joined_ref[c].astype(jnp.float32)
-        wide_ref[pl.ds(pl.multiple_of(c * 24, 8), 16), :] = value
-        return total + value
-
-    mean = lax.fori_loop(0, 128, total_of, zero, unroll=16) * (1 / 128)
-
-    def squares_of(c, total):
-        center = wide_ref[pl.ds(pl.multiple_of(c * 24, 8), 16), :] - mean
-        return total + center * center
-
-    scale = lax.rsqrt(lax.fori_loop(0, 128, squares_of, zero, unroll=16) * (1 / 128) + EPS)
+    base = joined_ref[0].astype(jnp.float32)
+
+    def totals_of(c, totals):
+        shifted = joined_ref[c].astype(jnp.float32) - base
+        wide_ref[pl.ds(pl.multiple_of(c * 24, 8), 16), :] = shifted
+        return totals[0] + shifted, totals[1] + shifted * shifted
+
+    total, squares = lax.fori_loop(0, 128, totals_of, (zero, zero), unroll=16)
+    mean = total * (1 / 128)
+    scale = lax.rsqrt(jnp.maximum(squares * (1 / 128) - mean * mean, 0.0) + EPS)
+    gate_copy(step).wait()
     for i in range(16):
         tile = wide_ref[pl.ds(i, 128, stride=24), :]
         tile = ((tile - mean[i : i + 1]) * scale[i : i + 1] * gain + bias).astype(jnp.bfloat16)
         value = lax.dot_general(tile, w_ref[...], (((0,), (0,)), ((), ())), preferred_element_type=jnp.float32)
-        out_ref[i] = (gate_ref[i * 128 : (i + 1) * 128, :] * value).astype(jnp.bfloat16)
+        gate = gate_ref[pl.ds(pl.multiple_of(step * 2048 + i * 128, 128), 128), :]
+        out_ref[i] = (gate * value).astype(jnp.bfloat16)
 
 
 def shards(
@@ -255,13 +265,13 @@
     core = lax.axis_index("core").astype(jnp.int32).reshape(1)
     joined = pl.pallas_call(
         join_kernel,
-        grid=(4,),
+        grid=(2,),
         in_specs=[
             pl.BlockSpec(memory_space=pltpu.SMEM),
             pl.BlockSpec(memory_space=pltpu.VMEM),
             pl.BlockSpec(memory_space=pltpu.VMEM),
         ],
-        out_specs=pl.BlockSpec((32, 64, 128), lambda b: (b, 0, 0)),
+        out_specs=pl.BlockSpec((64, 64, 128), lambda b: (b, 0, 0)),
         out_shape=HBM((128, 64, 128), jnp.bfloat16),
         scratch_shapes=[pltpu.VMEM((512, 1024), jnp.bfloat16), pltpu.VMEM((512, 1024), jnp.bfloat16)],
         compiler_params=params,
@@ -275,14 +285,18 @@
         grid=(4,),
         in_specs=[
             pl.BlockSpec((128, 16, 128), lambda b: (0, b, 0)),
-            pl.BlockSpec((2048, 128), lambda b: (b, 0)),
+            hbm,
             pl.BlockSpec((128, 1), lambda b: (0, 0)),
             pl.BlockSpec((128, 1), lambda b: (0, 0)),
             pl.BlockSpec((128, 128), lambda b: (0, 0)),
         ],
         out_specs=pl.BlockSpec((16, 128, 128), lambda b: (b, 0, 0)),
         out_shape=jax.ShapeDtypeStruct((64, 128, 128), jnp.bfloat16),
-        scratch_shapes=[pltpu.VMEM((128 * 24, 128), jnp.float32)],
+        scratch_shapes=[
+            pltpu.VMEM((128 * 24, 128), jnp.float32),
+            pltpu.VMEM((8192, 128), jnp.float32),
+            pltpu.SemaphoreType.DMA((4,)),
+        ],
         compiler_params=params,
         cost_estimate=pl.CostEstimate(flops=2 * 8192 * 128 * 128, bytes_accessed=8 << 20, transcendentals=0),
     )(home, pltpu.with_memory_space_constraint(gate, HBM), out_gain.reshape(128, 1), out_bias.reshape(128, 1), w_out)

time: 134 us -> 132 us (0.985)
  Pallas kernels: 23.4 us -> 21.6 us
where the time goes in v3:
time: 132 us; the launch traced here: 131 us
  blocking collectives  56.5 us (43%)
  waiting for transfers between devices  42.5 us (32%)
  Pallas kernels  21.6 us (16%)
  starting transfers between devices  8.89 us (7%)
  local copies, waits for them, and re-layouts  1.87 us (1%)
    all_to_all x1, blocking collectives, shards(): lax.all_to_all(packed, CHIPS, split_axis=0, concat_axis=0, tiled=True)  56.5 us
    all_to_all x1, waiting for transfers between devices, shards(): lax.all_to_all(joined, CHIPS, split_axis=0, concat_axis=0, tiled=True)  41 us
    pallas_call x1, Pallas kernels, shards(): pl.pallas_call(gate_kernel, grid=(16,), in_specs=[pl.BlockSpec((4, 128, 1...  8.87 us
    all_to_all x1, starting transfers between devices, shards(): lax.all_to_all(joined, CHIPS, split_axis=0, concat_axis=0, tiled=True)  6.5 us
    pallas_call x1, Pallas kernels, shards(): pl.pallas_call(epilogue_kernel, grid=(4,), in_specs=[pl.BlockSpec((128, 1...  4.88 us
    pallas_call x1, Pallas kernels, shards(): pl.pallas_call(prologue_kernel, in_specs=[hbm] * 7, out_shape=jax.ShapeDt...  4.63 us
    pallas_call x1, Pallas kernels, shards(): pl.pallas_call(join_kernel, grid=(2,), in_specs=[pl.BlockSpec(memory_spac...  3.21 us
  transfers between devices with their start and end apart: 2, of which 2 were waited for; matrix products, arithmetic and copies ran while one was open for 0% of the time, Pallas kernels for 7%

profile of v3, /device:TPU:1, one launch (start us, length us, event | category | flops | bytes accessed | tf_op | source)
XLA Modules:
  0.0 131.4 jit_solution(4040045285834850877)
XLA Ops:
  0.0 4.6 %shard_map.118 = bf16[128,48,128]{2,1,0:T(8,128)(2,1)S(1)} custom-call(bf16[64,32,128]{2,1,0:T(8,128)(2,1)} %left_hbm.1, bf16[128,32,128]{2,1,0:T(8,128)(2,1)} %right_hbm.1, s32[32,64]{1,0:T(8,128)} %bitcast.11, s32[32,128]{1,0:T(8,128)} %bitcast.12, f32[1,128]{1,0:T(1,128)} %bitcast.7, f32[1,128]{1,0:T(1,128)} %bitcast.9, bf16[128,512]{1,0:T(8,128)(2,1)} %w_hbm.1), custom_call_target="tpu_custom_call" | custom-call | flops 402653184 | bytes 3145728 | tf_op jit(solution)/shard_map/pallas_call | solution.py:226
  4.6 56.5 %all_to_all.10.own_ref = bf16[128,48,128]{2,1,0:T(8,128)(2,1)S(1)} all-to-all(bf16[128,48,128]{2,1,0:T(8,128)(2,1)S(1)} %shard_map.118), channel_id=1, replica_groups=mesh['x'=4,'zl'=4,'zh'=2,'y'=4,'core'=2] {'x','zl','zh','y'}, dimensions={0} | all-to-all | bytes 3145728 | tf_op jit(solution)/shard_map/all_to_all | solution.py:247
  61.1 2.4 %collective-permute-start = (bf16[128,16,128]{2,1,0:T(8,128)(2,1)S(1)}, bf16[128,16,128]{2,1,0:T(8,128)(2,1)S(1)}, u32[]{:S(2)}, u32[]{:S(2)}) collective-permute-start(bf16[128,16,128]{2,1,0:T(8,128)(2,1)S(1)} %slice.4), channel_id=1, source_target_pairs={{0,1},{1,0},{2,3},{3,2},{4,5},{5,4},{6,7},{7,6},{8,9},{9,8},{10,11... | collective-permute-start | bytes 1572872 | tf_op jit(solution)/shard_map/ppermute | solution.py:264
  63.5 1.5 %collective-permute-done.other_ref = bf16[128,16,128]{2,1,0:T(8,128)(2,1)S(1)} collective-permute-done((bf16[128,16,128]{2,1,0:T(8,128)(2,1)S(1)}, bf16[128,16,128]{2,1,0:T(8,128)(2,1)S(1)}, u32[]{:S(2)}, u32[]{:S(2)}) %collective-permute-start) | collective-permute-done | bytes 524320 | tf_op jit(solution)/shard_map/ppermute | solution.py:264
  65.1 3.2 %shard_map.119 = bf16[128,64,128]{2,1,0:T(8,128)(2,1)} custom-call(s32[1]{0:T(128)} %bitcast.core_ref, bf16[128,48,128]{2,1,0:T(8,128)(2,1)S(1)} %all_to_all.10.own_ref, bf16[128,16,128]{2,1,0:T(8,128)(2,1)S(1)} %collective-permute-done.other_ref), custom_call_target="tpu_custom_call" | custom-call | flops 1073741824 | bytes 4194304 | tf_op jit(solution)/shard_map/pallas_call | solution.py:266
  68.3 0.0 copy-start.5
  68.3 0.0 copy-start.6
  68.3 0.0 copy-start.1
  68.3 0.0 copy-start.3
  68.3 0.0 copy-start.4
  68.3 6.5 %all-to-all-start.1 = ((bf16[128,64,128]{2,1,0:T(8,128)(2,1)}), bf16[128,64,128]{2,1,0:T(8,128)(2,1)S(1)}, u32[]{:S(2)}, u32[]{:S(2)}) async-start(bf16[128,64,128]{2,1,0:T(8,128)(2,1)} %shard_map.119), calls=%async_computation.1 | async-start | bytes 4194304 | tf_op jit(solution)/shard_map/all_to_all | solution.py:281
  74.8 0.0 copy-done.5
  74.8 0.1 copy.13.gain_ref
  74.9 0.0 copy-done.6
  74.9 0.1 copy.14.bias_ref
  75.1 0.0 copy-done.1
  75.1 0.0 copy-done.3
  75.1 0.0 copy-done.4
  75.1 0.0 copy-start
  75.1 1.6 %copy-done = bf16[64,128,128]{2,1,0:T(8,128)(2,1)S(1)} copy-done((bf16[64,128,128]{2,1,0:T(8,128)(2,1)S(1)}, bf16[64,128,128]{2,1,0:T(8,128)(2,1)}, u32[]{:S(2)}) %copy-start) | copy-done | bytes 2097176
  76.7 8.9 %shard_map.120.gate_hbm = f32[8192,128]{1,0:T(8,128)} custom-call(bf16[64,128,128]{2,1,0:T(8,128)(2,1)S(1)} %copy-done, f32[1,128]{1,0:T(1,128)S(1)} %bitcast.8, f32[1,128]{1,0:T(1,128)S(1)} %bitcast.10, bf16[128,128]{1,0:T(8,128)(2,1)S(1)} %copy-done.1), custom_call_target="tpu_custom_call" | custom-call | flops 268435456 | bytes 6291456 | tf_op jit(solution)/shard_map/pallas_call | solution.py:249
  85.5 41.0 %all-to-all-done.1.joined_ref = bf16[128,64,128]{2,1,0:T(8,128)(2,1)S(1)} async-done(((bf16[128,64,128]{2,1,0:T(8,128)(2,1)}), bf16[128,64,128]{2,1,0:T(8,128)(2,1)S(1)}, u32[]{:S(2)}, u32[]{:S(2)}) %all-to-all-start.1) | async-done | bytes 2097184 | tf_op jit(solution)/shard_map/all_to_all | solution.py:281
  126.5 0.0 copy-done.2
  126.5 4.9 %shard_map.121 = bf16[64,128,128]{2,1,0:T(8,128)(2,1)} custom-call(bf16[128,64,128]{2,1,0:T(8,128)(2,1)S(1)} %all-to-all-done.1.joined_ref, f32[8192,128]{1,0:T(8,128)} %shard_map.120.gate_hbm, f32[128,1]{1,0:T(8,128)S(1)} %copy.13.gain_ref, f32[128,1]{1,0:T(8,128)S(1)} %copy.14.bias_ref, bf16[128,128]{1,0:T(8,128)(2,1)S(1)} %copy-done.2), custom_call_target="tpu_custom_call" | custom-call | flops 268435456 | bytes 8388608 | tf_op jit(solution)/shard_map/pallas_call | solution.py:283
  (2 shorter events, 0.0 us)
Async XLA Ops:
  61.1 3.9 %collective-permute-start = (bf16[128,16,128]{2,1,0:T(8,128)(2,1)S(1)}, bf16[128,16,128]{2,1,0:T(8,128)(2,1)S(1)}, u32[]{:S(2)}, u32[]{:S(2)}) collective-permute-start(bf16[128,16,128]{2,1,0:T(8,128)(2,1)S(1)} %slice.4), channel_id=1, source_target_pairs={{0,1},{1,0},{2,3},{3,2},{4,5},{5,4},{6,7},{7,6},{8,9},{9,8},{10,11... | collective-permute-start | bytes 1572872 | tf_op jit(solution)/shard_map/ppermute | solution.py:264
  68.3 6.5 %copy-start.5 = (f32[128]{0:T(128)S(1)}, f32[128]{0:T(128)}, u32[]{:S(2)}) copy-start(f32[128]{0:T(128)} %param.20) | copy-start | bytes 1540
  68.3 6.7 %copy-start.6 = (f32[128]{0:T(128)S(1)}, f32[128]{0:T(128)}, u32[]{:S(2)}) copy-start(f32[128]{0:T(128)} %param.21) | copy-start | bytes 1540
  68.3 6.8 %copy-start.1 = (bf16[128,128]{1,0:T(8,128)(2,1)S(1)}, bf16[128,128]{1,0:T(8,128)(2,1)}, u32[]{:S(2)}) copy-start(bf16[128,128]{1,0:T(8,128)(2,1)} %w_ref.2) | copy-start | bytes 98308
  68.3 6.8 %copy-start.3 = (f32[128]{0:T(128)S(1)}, f32[128]{0:T(128)}, u32[]{:S(2)}) copy-start(f32[128]{0:T(128)} %param.17) | copy-start | bytes 1540
  68.3 6.8 %copy-start.4 = (f32[128]{0:T(128)S(1)}, f32[128]{0:T(128)}, u32[]{:S(2)}) copy-start(f32[128]{0:T(128)} %param.18) | copy-start | bytes 1540
  68.3 58.2 %all-to-all-start.1 = ((bf16[128,64,128]{2,1,0:T(8,128)(2,1)}), bf16[128,64,128]{2,1,0:T(8,128)(2,1)S(1)}, u32[]{:S(2)}, u32[]{:S(2)}) async-start(bf16[128,64,128]{2,1,0:T(8,128)(2,1)} %shard_map.119), calls=%async_computation.1 | async-start | bytes 4194304 | tf_op jit(solution)/shard_map/all_to_all | solution.py:281
  75.1 1.6 %copy-start = (bf16[64,128,128]{2,1,0:T(8,128)(2,1)S(1)}, bf16[64,128,128]{2,1,0:T(8,128)(2,1)}, u32[]{:S(2)}) copy-start(bf16[64,128,128]{2,1,0:T(8,128)(2,1)} %pair_ref.1) | copy-start | bytes 6291460
  76.7 49.8 %copy-start.2 = (bf16[128,128]{1,0:T(8,128)(2,1)S(1)}, bf16[128,128]{1,0:T(8,128)(2,1)}, u32[]{:S(2)}) copy-start(bf16[128,128]{1,0:T(8,128)(2,1)} %w_ref.3) | copy-start | bytes 98308

commit v4 on v3

--- a/solution.py
+++ b/solution.py
@@ -28,7 +28,9 @@
     gain_hbm,
     bias_hbm,
     w_hbm,
-    out_ref,
+    out_hbm,
+    right_out_ref,
+    left_out_ref,
     left_ref,
     right_ref,
     mask_left_ref,
@@ -53,6 +55,15 @@
         pltpu.make_async_copy(mask_left_hbm, mask_left_ref, sems.at[6]),
     ]
     left_copy = pltpu.make_async_copy(left_hbm, left_ref, sems.at[7])
+    out_copies = [
+        pltpu.make_async_copy(
+            source.at[pl.ds(half * 64, 64)],
+            out_hbm.at[pl.ds(half * 64, 64), pl.ds(low, depth), :],
+            sems.at[8 + part * 2 + half],
+        )
+        for part, (source, low, depth) in enumerate(((right_out_ref, 0, 32), (left_out_ref, 32, 16)))
+        for half in range(2)
+    ]
     right_copies[0].start()
     for copy in small_copies:
         copy.start()
@@ -95,10 +106,12 @@
     def right_out(b, carry):
         for q in range(8):
             row = pl.multiple_of((b * 8 + q) * PITCH, 8)
-            out_ref[b * 8 + q, 0:32, :] = turned_ref[pl.ds(row, 32), :].astype(jnp.bfloat16)
-        return carry
-
-    lax.fori_loop(0, 16, right_out, 0, unroll=4)
+            right_out_ref[b * 8 + q] = turned_ref[pl.ds(row, 32), :].astype(jnp.bfloat16)
+        return carry
+
+    for half in range(2):
+        lax.fori_loop(half * 8, half * 8 + 8, right_out, 0, unroll=4)
+        out_copies[half].start()
 
     small_copies[4].wait()
     mask_left = mask_left_ref[...].astype(jnp.float32)
@@ -119,10 +132,14 @@
     def left_out(b, carry):
         for q in range(8):
             row = pl.multiple_of((b * 8 + q) * 24, 8)
-            out_ref[b * 8 + q, 32:48, :] = turned_ref[pl.ds(row, 16), :].astype(jnp.bfloat16)
-        return carry
-
-    lax.fori_loop(0, 16, left_out, 0, unroll=4)
+            left_out_ref[b * 8 + q] = turned_ref[pl.ds(row, 16), :].astype(jnp.bfloat16)
+        return carry
+
+    for half in range(2):
+        lax.fori_loop(half * 8, half * 8 + 8, left_out, 0, unroll=4)
+        out_copies[2 + half].start()
+    for copy in out_copies:
+        copy.wait()
 
 
 def join_kernel(core_ref, own_ref, other_ref, out_ref, left_ref, right_ref):
@@ -183,8 +200,8 @@
         for part in range(4):
             gate_copy(part).start()
 
-    gain = jnp.broadcast_to(gain_ref[...], (128, 128))
-    bias = jnp.broadcast_to(bias_ref[...], (128, 128))
+    gain = jnp.broadcast_to(gain_ref[...], (128, 128)).T
+    bias = jnp.broadcast_to(bias_ref[...], (128, 128)).T
     zero = jnp.zeros((16, 128), jnp.float32)
     base = joined_ref[0].astype(jnp.float32)
 
@@ -226,8 +243,11 @@
     packed = pl.pallas_call(
         prologue_kernel,
         in_specs=[hbm] * 7,
-        out_shape=jax.ShapeDtypeStruct((128, 48, 128), jnp.bfloat16),
+        out_specs=hbm,
+        out_shape=HBM((128, 48, 128), jnp.bfloat16),
         scratch_shapes=[
+            pltpu.VMEM((128, 32, 128), jnp.bfloat16),
+            pltpu.VMEM((128, 16, 128), jnp.bfloat16),
             pltpu.VMEM((64, 32, 128), jnp.bfloat16),
             pltpu.VMEM((128, 32, 128), jnp.bfloat16),
             pltpu.VMEM((32, 64), jnp.int32),
@@ -235,10 +255,10 @@
             pltpu.VMEM((1, 128), jnp.float32),
             pltpu.VMEM((1, 128), jnp.float32),
             pltpu.VMEM((128, 512), jnp.bfloat16),
-            pltpu.VMEM((128 * PITCH, 128), jnp.float32),
-            pltpu.VMEM((128 * PITCH, 128), jnp.float32),
+            pltpu.VMEM((129 * PITCH, 128), jnp.float32),
+            pltpu.VMEM((129 * PITCH, 128), jnp.float32),
             pltpu.VMEM((16, 128), jnp.float32),
-            pltpu.SemaphoreType.DMA((8,)),
+            pltpu.SemaphoreType.DMA((12,)),
         ],
         compiler_params=params,
         cost_estimate=pl.CostEstimate(flops=2 * 6144 * 128 * 256, bytes_accessed=3 << 20, transcendentals=6144 * 128),
@@ -261,6 +281,7 @@
         cost_estimate=pl.CostEstimate(flops=2 * 8192 * 128 * 128, bytes_accessed=6 << 20, transcendentals=8192 * 128),
     )(pair_block, gain_row, bias_row, w_gate_out)
 
+    mine, gate = lax.optimization_barrier((mine, gate))
     other_left = lax.ppermute(mine[:, 32:48, :], "core", [(0, 1), (1, 0)])
     core = lax.axis_index("core").astype(jnp.int32).reshape(1)
     joined = pl.pallas_call(
@@ -272,7 +293,7 @@
             pl.BlockSpec(memory_space=pltpu.VMEM),
         ],
         out_specs=pl.BlockSpec((64, 64, 128), lambda b: (b, 0, 0)),
-        out_shape=HBM((128, 64, 128), jnp.bfloat16),
+        out_shape=jax.ShapeDtypeStruct((128, 64, 128), jnp.bfloat16),
         scratch_shapes=[pltpu.VMEM((512, 1024), jnp.bfloat16), pltpu.VMEM((512, 1024), jnp.bfloat16)],
         compiler_params=params,
         cost_estimate=pl.CostEstimate(flops=2 * 1024 * 1024 * 512, bytes_accessed=4 << 20, transcendentals=0),
@@ -286,20 +307,20 @@
         in_specs=[
             pl.BlockSpec((128, 16, 128), lambda b: (0, b, 0)),
             hbm,
-            pl.BlockSpec((128, 1), lambda b: (0, 0)),
-            pl.BlockSpec((128, 1), lambda b: (0, 0)),
+            pl.BlockSpec((1, 128), lambda b: (0, 0)),
+            pl.BlockSpec((1, 128), lambda b: (0, 0)),
             pl.BlockSpec((128, 128), lambda b: (0, 0)),
         ],
         out_specs=pl.BlockSpec((16, 128, 128), lambda b: (b, 0, 0)),
         out_shape=jax.ShapeDtypeStruct((64, 128, 128), jnp.bfloat16),
         scratch_shapes=[
-            pltpu.VMEM((128 * 24, 128), jnp.float32),
+            pltpu.VMEM((129 * 24, 128), jnp.float32),
             pltpu.VMEM((8192, 128), jnp.float32),
             pltpu.SemaphoreType.DMA((4,)),
         ],
         compiler_params=params,
         cost_estimate=pl.CostEstimate(flops=2 * 8192 * 128 * 128, bytes_accessed=8 << 20, transcendentals=0),
-    )(home, pltpu.with_memory_space_constraint(gate, HBM), out_gain.reshape(128, 1), out_bias.reshape(128, 1), w_out)
+    )(home, pltpu.with_memory_space_constraint(gate, HBM), out_gain.reshape(1, 128), out_bias.reshape(1, 128), w_out)
 
 
 def solution(mesh):

time: 132 us -> 132 us (level)
  waiting for transfers between devices: 42.5 us -> 31.4 us
  starting transfers between devices: 8.89 us -> 18.9 us
  blocking collectives: 56.5 us -> 58 us
    all_to_all x1, waiting for transfers between devices: 41 us -> 29.8 us  [shards(): lax.all_to_all(packed, CHIPS, split_axis=0, concat_axis=0, tiled=True)]
    all_to_all x1, starting transfers between devices: 6.5 us -> 16.5 us  [shards(): lax.all_to_all(packed, CHIPS, split_axis=0, concat_axis=0, tiled=True)]
    all_to_all x1, blocking collectives: 56.5 us -> 58 us  [shards(): lax.all_to_all(joined, CHIPS, split_axis=0, concat_axis=0, tiled=True)]
where the time goes in v4:
time: 132 us; the launch traced here: 131 us
  blocking collectives  58 us (44%)
  waiting for transfers between devices  31.4 us (24%)
  Pallas kernels  21.5 us (16%)
  starting transfers between devices  18.9 us (14%)
  local copies, waits for them, and re-layouts  1.66 us (1%)
    all_to_all x1, blocking collectives, shards(): lax.all_to_all(joined, CHIPS, split_axis=0, concat_axis=0, tiled=True)  58 us
    all_to_all x1, waiting for transfers between devices, shards(): lax.all_to_all(packed, CHIPS, split_axis=0, concat_axis=0, tiled=True)  29.8 us
    all_to_all x1, starting transfers between devices, shards(): lax.all_to_all(packed, CHIPS, split_axis=0, concat_axis=0, tiled=True)  16.5 us
    pallas_call x1, Pallas kernels, shards(): pl.pallas_call(gate_kernel, grid=(16,), in_specs=[pl.BlockSpec((4, 128, 1...  8.87 us
    pallas_call x1, Pallas kernels, shards(): pl.pallas_call(prologue_kernel, in_specs=[hbm] * 7, out_specs=hbm, out_sh...  5.43 us
    pallas_call x1, Pallas kernels, shards(): pl.pallas_call(epilogue_kernel, grid=(4,), in_specs=[pl.BlockSpec((128, 1...  4.91 us
  transfers between devices with their start and end apart: 2, of which 2 were waited for; matrix products, arithmetic and copies ran while one was open for 0% of the time, Pallas kernels for 7%

profile of v4, /device:TPU:1, one launch (start us, length us, event | category | flops | bytes accessed | tf_op | source)
XLA Modules:
  0.0 131.5 jit_solution(2751654681045872861)
XLA Ops:
  0.0 5.4 %shard_map.118 = bf16[128,48,128]{2,1,0:T(8,128)(2,1)} custom-call(bf16[64,32,128]{2,1,0:T(8,128)(2,1)} %left_hbm.1, bf16[128,32,128]{2,1,0:T(8,128)(2,1)} %right_hbm.1, s32[32,64]{1,0:T(8,128)} %bitcast.13, s32[32,128]{1,0:T(8,128)} %bitcast.14, f32[1,128]{1,0:T(1,128)} %bitcast.7, f32[1,128]{1,0:T(1,128)} %bitcast.9, bf16[128,512]{1,0:T(8,128)(2,1)} %w_hbm.1), custom_call_target="tpu_custom_call" | custom-call | flops 402653184 | bytes 3145728 | tf_op jit(solution)/shard_map/pallas_call | solution.py:243
  5.4 0.0 copy-start.1
  5.5 0.0 copy-start.3
  5.5 0.0 copy-start.4
  5.5 16.5 %all-to-all-start = ((bf16[128,48,128]{2,1,0:T(8,128)(2,1)}), bf16[128,48,128]{2,1,0:T(8,128)(2,1)S(1)}, u32[]{:S(2)}, u32[]{:S(2)}) async-start(bf16[128,48,128]{2,1,0:T(8,128)(2,1)} %shard_map.118), calls=%async_computation | async-start | bytes 3145728 | tf_op jit(solution)/shard_map/all_to_all | solution.py:267
  22.0 0.0 copy-done.1
  22.0 0.0 copy-done.3
  22.0 0.0 copy-done.4
  22.0 0.0 copy-start
  22.0 1.6 %copy-done = bf16[64,128,128]{2,1,0:T(8,128)(2,1)S(1)} copy-done((bf16[64,128,128]{2,1,0:T(8,128)(2,1)S(1)}, bf16[64,128,128]{2,1,0:T(8,128)(2,1)}, u32[]{:S(2)}) %copy-start) | copy-done | bytes 2097176
  23.6 8.9 %shard_map.119.gate_hbm = f32[8192,128]{1,0:T(8,128)} custom-call(bf16[64,128,128]{2,1,0:T(8,128)(2,1)S(1)} %copy-done, f32[1,128]{1,0:T(1,128)S(1)} %bitcast.8, f32[1,128]{1,0:T(1,128)S(1)} %bitcast.10, bf16[128,128]{1,0:T(8,128)(2,1)S(1)} %copy-done.1), custom_call_target="tpu_custom_call" | custom-call | flops 268435456 | bytes 6291456 | tf_op jit(solution)/shard_map/pallas_call | solution.py:269
  32.5 29.8 %all-to-all-done.own_ref = bf16[128,48,128]{2,1,0:T(8,128)(2,1)S(1)} async-done(((bf16[128,48,128]{2,1,0:T(8,128)(2,1)}), bf16[128,48,128]{2,1,0:T(8,128)(2,1)S(1)}, u32[]{:S(2)}, u32[]{:S(2)}) %all-to-all-start) | async-done | bytes 1572896 | tf_op jit(solution)/shard_map/all_to_all | solution.py:267
  62.3 2.4 %collective-permute-start = (bf16[128,16,128]{2,1,0:T(8,128)(2,1)S(1)}, bf16[128,16,128]{2,1,0:T(8,128)(2,1)S(1)}, u32[]{:S(2)}, u32[]{:S(2)}) collective-permute-start(bf16[128,16,128]{2,1,0:T(8,128)(2,1)S(1)} %slice.3), channel_id=1, source_target_pairs={{0,1},{1,0},{2,3},{3,2},{4,5},{5,4},{6,7},{7,6},{8,9},{9,8},{10,11... | collective-permute-start | bytes 1572872 | tf_op jit(solution)/shard_map/ppermute | solution.py:285
  64.7 1.5 %collective-permute-done.other_ref = bf16[128,16,128]{2,1,0:T(8,128)(2,1)S(1)} collective-permute-done((bf16[128,16,128]{2,1,0:T(8,128)(2,1)S(1)}, bf16[128,16,128]{2,1,0:T(8,128)(2,1)S(1)}, u32[]{:S(2)}, u32[]{:S(2)}) %collective-permute-start) | collective-permute-done | bytes 524320 | tf_op jit(solution)/shard_map/ppermute | solution.py:285
  66.3 2.2 %shard_map.120 = bf16[128,64,128]{2,1,0:T(8,128)(2,1)S(1)} custom-call(s32[1]{0:T(128)} %bitcast.core_ref, bf16[128,48,128]{2,1,0:T(8,128)(2,1)S(1)} %all-to-all-done.own_ref, bf16[128,16,128]{2,1,0:T(8,128)(2,1)S(1)} %collective-permute-done.other_ref), custom_call_target="tpu_custom_call" | custom-call | flops 1073741824 | bytes 4194304 | tf_op jit(solution)/shard_map/pallas_call | solution.py:287
  68.5 0.0 copy-start.2
  68.5 0.0 copy-start.5
  68.5 0.0 copy-start.6
  68.6 58.0 %all_to_all.10.joined_ref = bf16[128,64,128]{2,1,0:T(8,128)(2,1)S(1)} all-to-all(bf16[128,64,128]{2,1,0:T(8,128)(2,1)S(1)} %shard_map.120), channel_id=1, replica_groups=mesh['x'=4,'zl'=4,'zh'=2,'y'=4,'core'=2] {'x','zl','zh','y'}, dimensions={0} | all-to-all | bytes 4194304 | tf_op jit(solution)/shard_map/all_to_all | solution.py:302
  126.5 0.0 copy-done.2
  126.5 0.0 copy-done.5
  126.5 0.0 copy-done.6
  126.6 4.9 %shard_map.121 = bf16[64,128,128]{2,1,0:T(8,128)(2,1)} custom-call(bf16[128,64,128]{2,1,0:T(8,128)(2,1)S(1)} %all_to_all.10.joined_ref, f32[8192,128]{1,0:T(8,128)} %shard_map.119.gate_hbm, f32[1,128]{1,0:T(1,128)S(1)} %bitcast.11, f32[1,128]{1,0:T(1,128)S(1)} %bitcast.12, bf16[128,128]{1,0:T(8,128)(2,1)S(1)} %copy-done.2), custom_call_target="tpu_custom_call" | custom-call | flops 268435456 | bytes 8388608 | tf_op jit(solution)/shard_map/pallas_call | solution.py:304
  (1 shorter events, 0.0 us)
Async XLA Ops:
  5.4 16.5 %copy-start.1 = (bf16[128,128]{1,0:T(8,128)(2,1)S(1)}, bf16[128,128]{1,0:T(8,128)(2,1)}, u32[]{:S(2)}) copy-start(bf16[128,128]{1,0:T(8,128)(2,1)} %w_ref.2) | copy-start | bytes 98308
  5.5 16.5 %copy-start.3 = (f32[128]{0:T(128)S(1)}, f32[128]{0:T(128)}, u32[]{:S(2)}) copy-start(f32[128]{0:T(128)} %param.17) | copy-start | bytes 1540
  5.5 16.5 %copy-start.4 = (f32[128]{0:T(128)S(1)}, f32[128]{0:T(128)}, u32[]{:S(2)}) copy-start(f32[128]{0:T(128)} %param.18) | copy-start | bytes 1540
  5.5 56.8 %all-to-all-start = ((bf16[128,48,128]{2,1,0:T(8,128)(2,1)}), bf16[128,48,128]{2,1,0:T(8,128)(2,1)S(1)}, u32[]{:S(2)}, u32[]{:S(2)}) async-start(bf16[128,48,128]{2,1,0:T(8,128)(2,1)} %shard_map.118), calls=%async_computation | async-start | bytes 3145728 | tf_op jit(solution)/shard_map/all_to_all | solution.py:267
  22.0 1.6 %copy-start = (bf16[64,128,128]{2,1,0:T(8,128)(2,1)S(1)}, bf16[64,128,128]{2,1,0:T(8,128)(2,1)}, u32[]{:S(2)}) copy-start(bf16[64,128,128]{2,1,0:T(8,128)(2,1)} %pair_ref.1) | copy-start | bytes 6291460
  62.3 3.9 %collective-permute-start = (bf16[128,16,128]{2,1,0:T(8,128)(2,1)S(1)}, bf16[128,16,128]{2,1,0:T(8,128)(2,1)S(1)}, u32[]{:S(2)}, u32[]{:S(2)}) collective-permute-start(bf16[128,16,128]{2,1,0:T(8,128)(2,1)S(1)} %slice.3), channel_id=1, source_target_pairs={{0,1},{1,0},{2,3},{3,2},{4,5},{5,4},{6,7},{7,6},{8,9},{9,8},{10,11... | collective-permute-start | bytes 1572872 | tf_op jit(solution)/shard_map/ppermute | solution.py:285
  68.5 58.0 %copy-start.2 = (bf16[128,128]{1,0:T(8,128)(2,1)S(1)}, bf16[128,128]{1,0:T(8,128)(2,1)}, u32[]{:S(2)}) copy-start(bf16[128,128]{1,0:T(8,128)(2,1)} %w_ref.3) | copy-start | bytes 98308
  68.5 58.0 %copy-start.5 = (f32[128]{0:T(128)S(1)}, f32[128]{0:T(128)}, u32[]{:S(2)}) copy-start(f32[128]{0:T(128)} %param.20) | copy-start | bytes 1540
  68.5 58.0 %copy-start.6 = (f32[128]{0:T(128)S(1)}, f32[128]{0:T(128)}, u32[]{:S(2)}) copy-start(f32[128]{0:T(128)} %param.21) | copy-start | bytes 1540

commit v5 on v4

--- a/solution.py
+++ b/solution.py
@@ -142,40 +142,49 @@
         copy.wait()
 
 
-def join_kernel(core_ref, own_ref, other_ref, out_ref, left_ref, right_ref):
+def unfold_left(even, odd):
+    low_half = lax.broadcasted_iota(jnp.int32, (16, 128), 1) < 64
+    even = even.astype(jnp.float32)
+    odd = odd.astype(jnp.float32)
+    first = jnp.where(low_half, even, pltpu.roll(odd, 64, 1))
+    second = jnp.where(low_half, pltpu.roll(even, 64, 1), odd)
+    return jnp.concatenate([first, second], axis=0).astype(jnp.bfloat16)
+
+
+def layout_kernel(core_ref, own_ref, right_ref, left_ref):
     core = core_ref[0]
-    lane = lax.broadcasted_iota(jnp.int32, (16, 128), 1)
-    low_half = lane < 64
 
     def gather(t, carry):
+        row = pl.multiple_of(t * 32, 32)
         for side in range(2):
             block = 2 * t + (core if side == 0 else 1 - core)
-            row = pl.multiple_of((side * 8 + t) * 32, 32)
             for jb in range(8):
-                right_ref[pl.ds(row, 32), jb * 128 : (jb + 1) * 128] = own_ref[block * 8 + jb, 0:32, :]
-            for pair in range(8):
-                if side == 0:
-                    even = own_ref[pair * 16 + t, 32:48, :]
-                    odd = own_ref[pair * 16 + 8 + t, 32:48, :]
-                else:
-                    even = other_ref[pair * 16 + t]
-                    odd = other_ref[pair * 16 + 8 + t]
-                even = even.astype(jnp.float32)
-                odd = odd.astype(jnp.float32)
-                first = jnp.where(low_half, even, pltpu.roll(odd, 64, 1))
-                second = jnp.where(low_half, pltpu.roll(even, 64, 1), odd)
-                both = jnp.concatenate([first, second], axis=0).astype(jnp.bfloat16)
-                left_ref[pl.ds(row, 32), pair * 128 : (pair + 1) * 128] = both
-        return carry
-
+                right_ref[pl.ds(side * 256 + row, 32), jb * 128 : (jb + 1) * 128] = own_ref[block * 8 + jb, 0:32, :]
+        for pair in range(8):
+            left_ref[pl.ds(row, 32), pair * 128 : (pair + 1) * 128] = unfold_left(
+                own_ref[pair * 16 + t, 32:48, :], own_ref[pair * 16 + 8 + t, 32:48, :]
+            )
+        return carry
+
+    lax.fori_loop(0, 8, gather, 0, unroll=2)
+
+
+def join_kernel(own_left_ref, right_ref, other_ref, out_ref, left_ref):
     @pl.when(pl.program_id(0) == 0)
     def _():
+        def gather(t, carry):
+            row = pl.multiple_of(t * 32, 32)
+            for pair in range(8):
+                left_ref[pl.ds(row, 32), pair * 128 : (pair + 1) * 128] = unfold_left(
+                    other_ref[pair * 16 + t], other_ref[pair * 16 + 8 + t]
+                )
+            return carry
+
         lax.fori_loop(0, 8, gather, 0, unroll=2)
 
     column = pl.multiple_of(pl.program_id(0) * 512, 512)
-    total = lax.dot_general(
-        left_ref[:, pl.ds(column, 512)], right_ref[...], (((0,), (0,)), ((), ())), preferred_element_type=jnp.float32
-    )
+    lhs = jnp.concatenate([own_left_ref[:, pl.ds(column, 512)], left_ref[:, pl.ds(column, 512)]], axis=0)
+    total = lax.dot_general(lhs, right_ref[...], (((0,), (0,)), ((), ())), preferred_element_type=jnp.float32)
     for q in range(8):
         for jb in range(8):
             out_ref[q * 8 + jb] = total[q * 64 : (q + 1) * 64, jb * 128 : (jb + 1) * 128].astype(jnp.bfloat16)
@@ -284,20 +293,25 @@
     mine, gate = lax.optimization_barrier((mine, gate))
     other_left = lax.ppermute(mine[:, 32:48, :], "core", [(0, 1), (1, 0)])
     core = lax.axis_index("core").astype(jnp.int32).reshape(1)
+    vmem = pl.BlockSpec(memory_space=pltpu.VMEM)
+    right_matrix, own_left = pl.pallas_call(
+        layout_kernel,
+        in_specs=[pl.BlockSpec(memory_space=pltpu.SMEM), vmem],
+        out_specs=[vmem, vmem],
+        out_shape=[jax.ShapeDtypeStruct((512, 1024), jnp.bfloat16), jax.ShapeDtypeStruct((256, 1024), jnp.bfloat16)],
+        compiler_params=params,
+        cost_estimate=pl.CostEstimate(flops=1 << 20, bytes_accessed=3 << 20, transcendentals=0),
+    )(core, mine)
     joined = pl.pallas_call(
         join_kernel,
         grid=(2,),
-        in_specs=[
-            pl.BlockSpec(memory_space=pltpu.SMEM),
-            pl.BlockSpec(memory_space=pltpu.VMEM),
-            pl.BlockSpec(memory_space=pltpu.VMEM),
-        ],
+        in_specs=[vmem, vmem, vmem],
         out_specs=pl.BlockSpec((64, 64, 128), lambda b: (b, 0, 0)),
         out_shape=jax.ShapeDtypeStruct((128, 64, 128), jnp.bfloat16),
-        scratch_shapes=[pltpu.VMEM((512, 1024), jnp.bfloat16), pltpu.VMEM((512, 1024), jnp.bfloat16)],
+        scratch_shapes=[pltpu.VMEM((256, 1024), jnp.bfloat16)],
         compiler_params=params,
         cost_estimate=pl.CostEstimate(flops=2 * 1024 * 1024 * 512, bytes_accessed=4 << 20, transcendentals=0),
-    )(core, mine, other_left)
+    )(own_left, right_matrix, other_left)
 
     home = lax.all_to_all(joined, CHIPS, split_axis=0, concat_axis=0, tiled=True)
 

time: 132 us -> 132 us (level)
  no operation moved by 1% of the time
where the time goes in v5:
time: 132 us; the launch traced here: 131 us
  blocking collectives  58 us (44%)
  waiting for transfers between devices  30.8 us (23%)
  Pallas kernels  21.8 us (17%)
  starting transfers between devices  18.9 us (14%)
  local copies, waits for them, and re-layouts  1.66 us (1%)
    all_to_all x1, blocking collectives, shards(): lax.all_to_all(joined, CHIPS, split_axis=0, concat_axis=0, tiled=True)  58 us
    all_to_all x1, waiting for transfers between devices, shards(): lax.all_to_all(packed, CHIPS, split_axis=0, concat_axis=0, tiled=True)  29.8 us
    all_to_all x1, starting transfers between devices, shards(): lax.all_to_all(packed, CHIPS, split_axis=0, concat_axis=0, tiled=True)  16.5 us
    pallas_call x1, Pallas kernels, shards(): pl.pallas_call(gate_kernel, grid=(16,), in_specs=[pl.BlockSpec((4, 128, 1...  8.9 us
    pallas_call x1, Pallas kernels, shards(): pl.pallas_call(prologue_kernel, in_specs=[hbm] * 7, out_specs=hbm, out_sh...  5.43 us
    pallas_call x1, Pallas kernels, shards(): pl.pallas_call(epilogue_kernel, grid=(4,), in_specs=[pl.BlockSpec((128, 1...  4.91 us
  transfers between devices with their start and end apart: 2, of which 2 were waited for; matrix products, arithmetic and copies ran while one was open for 0% of the time, Pallas kernels for 7%

profile of v5, /device:TPU:1, one launch (start us, length us, event | category | flops | bytes accessed | tf_op | source)
XLA Modules:
  0.0 131.2 jit_solution(2418466062588734208)
XLA Ops:
  0.0 5.4 %shard_map.118 = bf16[128,48,128]{2,1,0:T(8,128)(2,1)} custom-call(bf16[64,32,128]{2,1,0:T(8,128)(2,1)} %left_hbm.1, bf16[128,32,128]{2,1,0:T(8,128)(2,1)} %right_hbm.1, s32[32,64]{1,0:T(8,128)} %bitcast.13, s32[32,128]{1,0:T(8,128)} %bitcast.14, f32[1,128]{1,0:T(1,128)} %bitcast.7, f32[1,128]{1,0:T(1,128)} %bitcast.9, bf16[128,512]{1,0:T(8,128)(2,1)} %w_hbm.1), custom_call_target="tpu_custom_call" | custom-call | flops 402653184 | bytes 3145728 | tf_op jit(solution)/shard_map/pallas_call | solution.py:252
  5.4 0.0 copy-start.1
  5.5 0.0 copy-start.3
  5.5 0.0 copy-start.4
  5.5 16.5 %all-to-all-start = ((bf16[128,48,128]{2,1,0:T(8,128)(2,1)}), bf16[128,48,128]{2,1,0:T(8,128)(2,1)S(1)}, u32[]{:S(2)}, u32[]{:S(2)}) async-start(bf16[128,48,128]{2,1,0:T(8,128)(2,1)} %shard_map.118), calls=%async_computation | async-start | bytes 3145728 | tf_op jit(solution)/shard_map/all_to_all | solution.py:276
  22.0 0.0 copy-done.1
  22.0 0.0 copy-done.3
  22.0 0.0 copy-done.4
  22.0 0.0 copy-start
  22.0 1.6 %copy-done = bf16[64,128,128]{2,1,0:T(8,128)(2,1)S(1)} copy-done((bf16[64,128,128]{2,1,0:T(8,128)(2,1)S(1)}, bf16[64,128,128]{2,1,0:T(8,128)(2,1)}, u32[]{:S(2)}) %copy-start) | copy-done | bytes 2097176
  23.6 8.9 %shard_map.119.gate_hbm = f32[8192,128]{1,0:T(8,128)} custom-call(bf16[64,128,128]{2,1,0:T(8,128)(2,1)S(1)} %copy-done, f32[1,128]{1,0:T(1,128)S(1)} %bitcast.8, f32[1,128]{1,0:T(1,128)S(1)} %bitcast.10, bf16[128,128]{1,0:T(8,128)(2,1)S(1)} %copy-done.1), custom_call_target="tpu_custom_call" | custom-call | flops 268435456 | bytes 6291456 | tf_op jit(solution)/shard_map/pallas_call | solution.py:278
  32.5 29.8 %all-to-all-done.own_ref = bf16[128,48,128]{2,1,0:T(8,128)(2,1)S(1)} async-done(((bf16[128,48,128]{2,1,0:T(8,128)(2,1)}), bf16[128,48,128]{2,1,0:T(8,128)(2,1)S(1)}, u32[]{:S(2)}, u32[]{:S(2)}) %all-to-all-start) | async-done | bytes 1572896 | tf_op jit(solution)/shard_map/all_to_all | solution.py:276
  62.3 2.4 %collective-permute-start = (bf16[128,16,128]{2,1,0:T(8,128)(2,1)S(1)}, bf16[128,16,128]{2,1,0:T(8,128)(2,1)S(1)}, u32[]{:S(2)}, u32[]{:S(2)}) collective-permute-start(bf16[128,16,128]{2,1,0:T(8,128)(2,1)S(1)} %slice.3), channel_id=1, source_target_pairs={{0,1},{1,0},{2,3},{3,2},{4,5},{5,4},{6,7},{7,6},{8,9},{9,8},{10,11... | collective-permute-start | bytes 1572872 | tf_op jit(solution)/shard_map/ppermute | solution.py:294
  64.7 0.6 shard_map.120
  65.3 0.9 collective-permute-done.other_ref
  66.3 1.9 %shard_map.121 = bf16[128,64,128]{2,1,0:T(8,128)(2,1)S(1)} custom-call(bf16[256,1024]{1,0:T(8,128)(2,1)S(1)} %get-tuple-element.10.own_left_ref, bf16[512,1024]{1,0:T(8,128)(2,1)S(1)} %get-tuple-element.11.right_ref, bf16[128,16,128]{2,1,0:T(8,128)(2,1)S(1)} %collective-permute-done.other_ref), custom_call_target="tpu_custom_call" | custom-call | flops 1073741824 | bytes 4194304 | tf_op jit(solution)/shard_map/pallas_call | solution.py:305
  68.2 0.0 copy-start.2
  68.2 0.0 copy-start.5
  68.2 0.0 copy-start.6
  68.3 58.0 %all_to_all.10.joined_ref = bf16[128,64,128]{2,1,0:T(8,128)(2,1)S(1)} all-to-all(bf16[128,64,128]{2,1,0:T(8,128)(2,1)S(1)} %shard_map.121), channel_id=1, replica_groups=mesh['x'=4,'zl'=4,'zh'=2,'y'=4,'core'=2] {'x','zl','zh','y'}, dimensions={0} | all-to-all | bytes 4194304 | tf_op jit(solution)/shard_map/all_to_all | solution.py:316
  126.2 0.0 copy-done.2
  126.2 0.0 copy-done.5
  126.2 0.0 copy-done.6
  126.3 4.9 %shard_map.122 = bf16[64,128,128]{2,1,0:T(8,128)(2,1)} custom-call(bf16[128,64,128]{2,1,0:T(8,128)(2,1)S(1)} %all_to_all.10.joined_ref, f32[8192,128]{1,0:T(8,128)} %shard_map.119.gate_hbm, f32[1,128]{1,0:T(1,128)S(1)} %bitcast.11, f32[1,128]{1,0:T(1,128)S(1)} %bitcast.12, bf16[128,128]{1,0:T(8,128)(2,1)S(1)} %copy-done.2), custom_call_target="tpu_custom_call" | custom-call | flops 268435456 | bytes 8388608 | tf_op jit(solution)/shard_map/pallas_call | solution.py:318
  (1 shorter events, 0.0 us)
Async XLA Ops:
  5.4 16.5 %copy-start.1 = (bf16[128,128]{1,0:T(8,128)(2,1)S(1)}, bf16[128,128]{1,0:T(8,128)(2,1)}, u32[]{:S(2)}) copy-start(bf16[128,128]{1,0:T(8,128)(2,1)} %w_ref.2) | copy-start | bytes 98308
  5.5 16.5 %copy-start.3 = (f32[128]{0:T(128)S(1)}, f32[128]{0:T(128)}, u32[]{:S(2)}) copy-start(f32[128]{0:T(128)} %param.17) | copy-start | bytes 1540
  5.5 16.5 %copy-start.4 = (f32[128]{0:T(128)S(1)}, f32[128]{0:T(128)}, u32[]{:S(2)}) copy-start(f32[128]{0:T(128)} %param.18) | copy-start | bytes 1540
  5.5 56.8 %all-to-all-start = ((bf16[128,48,128]{2,1,0:T(8,128)(2,1)}), bf16[128,48,128]{2,1,0:T(8,128)(2,1)S(1)}, u32[]{:S(2)}, u32[]{:S(2)}) async-start(bf16[128,48,128]{2,1,0:T(8,128)(2,1)} %shard_map.118), calls=%async_computation | async-start | bytes 3145728 | tf_op jit(solution)/shard_map/all_to_all | solution.py:276
  22.0 1.6 %copy-start = (bf16[64,128,128]{2,1,0:T(8,128)(2,1)S(1)}, bf16[64,128,128]{2,1,0:T(8,128)(2,1)}, u32[]{:S(2)}) copy-start(bf16[64,128,128]{2,1,0:T(8,128)(2,1)} %pair_ref.1) | copy-start | bytes 6291460
  62.3 3.9 %collective-permute-start = (bf16[128,16,128]{2,1,0:T(8,128)(2,1)S(1)}, bf16[128,16,128]{2,1,0:T(8,128)(2,1)S(1)}, u32[]{:S(2)}, u32[]{:S(2)}) collective-permute-start(bf16[128,16,128]{2,1,0:T(8,128)(2,1)S(1)} %slice.3), channel_id=1, source_target_pairs={{0,1},{1,0},{2,3},{3,2},{4,5},{5,4},{6,7},{7,6},{8,9},{9,8},{10,11... | collective-permute-start | bytes 1572872 | tf_op jit(solution)/shard_map/ppermute | solution.py:294
  68.2 58.0 %copy-start.2 = (bf16[128,128]{1,0:T(8,128)(2,1)S(1)}, bf16[128,128]{1,0:T(8,128)(2,1)}, u32[]{:S(2)}) copy-start(bf16[128,128]{1,0:T(8,128)(2,1)} %w_ref.3) | copy-start | bytes 98308
  68.2 58.0 %copy-start.5 = (f32[128]{0:T(128)S(1)}, f32[128]{0:T(128)}, u32[]{:S(2)}) copy-start(f32[128]{0:T(128)} %param.20) | copy-start | bytes 1540
  68.2 58.0 %copy-start.6 = (f32[128]{0:T(128)S(1)}, f32[128]{0:T(128)}, u32[]{:S(2)}) copy-start(f32[128]{0:T(128)} %param.21) | copy-start | bytes 1540
